TPU v7x, 32 devices: a whole 2x2x4 slice. The times are simulated.
32 devices in a mesh: dp: 8 (over z, y), tensor: 4 (over x, core).
Axes of the slice: x: 2, y: 2, z: 4, core: 2. Of those that a mesh axis runs over, the one named last changes fastest.
Arguments:
- tokens: bfloat16 [8192, 768], P('dp'), may hold values from -6 to 6
- text: bfloat16 [32, 77, 768], P('dp'), may hold values from -6 to 6
- timesteps: int32 [32], P('dp'), may hold values from 0 to 999
- item_frames: int32 [32], P('dp'), may hold values from 0 to 1024, as said below
- cotangent: bfloat16 [8192, 768], P('dp'), may hold values from -6 to 6
- self_query: bfloat16 [2, 768, 768], P(None, None, 'tensor'), may hold values from -0.21875 to 0.21875
- self_query_bias: bfloat16 [2, 768], P(None, 'tensor'), may hold values from -3 to 3
- self_key: bfloat16 [2, 768, 768], P(None, None, 'tensor'), may hold values from -0.21875 to 0.21875
- self_value: bfloat16 [2, 768, 768], P(None, None, 'tensor'), may hold values from -0.21875 to 0.21875
- self_value_bias: bfloat16 [2, 768], P(None, 'tensor'), may hold values from -3 to 3
- self_output: bfloat16 [2, 768, 768], P(None, 'tensor'), may hold values from -0.875 to 0.875
- self_output_bias: bfloat16 [2, 768], replicated, may hold values from -2 to 2
- cross_query: bfloat16 [2, 768, 768], P(None, None, 'tensor'), may hold values from -0.21875 to 0.21875
- cross_query_bias: bfloat16 [2, 768], P(None, 'tensor'), may hold values from -3 to 3
- cross_key: bfloat16 [2, 768, 768], P(None, None, 'tensor'), may hold values from -0.21875 to 0.21875
- cross_value: bfloat16 [2, 768, 768], P(None, None, 'tensor'), may hold values from -0.21875 to 0.21875
- cross_value_bias: bfloat16 [2, 768], P(None, 'tensor'), may hold values from -3 to 3
- cross_output: bfloat16 [2, 768, 768], P(None, 'tensor'), may hold values from -0.21875 to 0.21875
- cross_output_bias: bfloat16 [2, 768], replicated, may hold values from -2 to 2
- hidden_up: bfloat16 [2, 768, 3072], P(None, None, 'tensor'), may hold values from -0.21875 to 0.21875
- hidden_up_bias: bfloat16 [2, 3072], P(None, 'tensor'), may hold values from -3 to 3
- hidden_down: bfloat16 [2, 3072, 768], P(None, 'tensor'), may hold values from -0.109375 to 0.109375
- hidden_down_bias: bfloat16 [2, 768], replicated, may hold values from -2 to 2
- modulation: bfloat16 [2, 768, 6912], P(None, None, 'tensor'), may hold values from -0.21875 to 0.21875
- modulation_bias: bfloat16 [2, 6912], P(None, 'tensor'), may hold values from -2 to 2
Outputs:
- output: bfloat16 [8192, 768], P('dp')
- input_grad: bfloat16 [8192, 768], P('dp')
- self_query_grad: float32 [2, 768, 768], P(None, 'dp', 'tensor')
- self_query_bias_grad: float32 [2, 768], P(None, 'tensor')
- self_key_grad: float32 [2, 768, 768], P(None, 'dp', 'tensor')
- self_value_grad: float32 [2, 768, 768], P(None, 'dp', 'tensor')
- self_value_bias_grad: float32 [2, 768], P(None, 'tensor')
- self_output_grad: float32 [2, 768, 768], P(None, 'tensor', 'dp')
- self_output_bias_grad: float32 [2, 768], P(None, 'dp')
- cross_query_grad: float32 [2, 768, 768], P(None, 'dp', 'tensor')
- cross_query_bias_grad: float32 [2, 768], P(None, 'tensor')
- cross_key_grad: float32 [2, 768, 768], P(None, 'dp', 'tensor')
- cross_value_grad: float32 [2, 768, 768], P(None, 'dp', 'tensor')
- cross_value_bias_grad: float32 [2, 768], P(None, 'tensor')
- cross_output_grad: float32 [2, 768, 768], P(None, 'tensor', 'dp')
- cross_output_bias_grad: float32 [2, 768], P(None, 'dp')
- hidden_up_grad: float32 [2, 768, 3072], P(None, 'dp', 'tensor')
- hidden_up_bias_grad: float32 [2, 3072], P(None, 'tensor')
- hidden_down_grad: float32 [2, 3072, 768], P(None, 'tensor', 'dp')
- hidden_down_bias_grad: float32 [2, 768], P(None, 'dp')
- modulation_grad: float32 [2, 768, 6912], P(None, 'dp', 'tensor')
- modulation_bias_grad: float32 [2, 6912], P(None, 'tensor')
Inputs may be any that keep to these rules, and one draw needn't show every extreme that they name: `item_frames`: each aligned block of 1024 frames of a dp index is filled exactly by whole items; the block's 1024 // 256 slots give their lengths in order, items first and zeros after; a length is 256, 512 or 1024; some block holds a single item of 1024 frames.
All inputs are finite; a program needn't handle non-finite values.
Results may differ from a plain program's by a relative error of at most 0.029.
Values may be sent and summed in bfloat16 or wider, within the bound.
No kernel may reach another device: no remote copies, remote signals or barrier semaphores. Data moves between devices by JAX's collectives and lax.ppermute only.
A program may use at most 256 MiB of HBM per device.

v0:
```python
from functools import partial
import math

import jax
import jax.numpy as jnp
from jax import lax
from jax.experimental import pallas as pl
from jax.experimental.pallas import tpu as pltpu
from jax.sharding import PartitionSpec as P

HEAD_WIDTH = 64
UNIT = 256
LAYERS = 2
WINDOW = 1024
EPSILON = 1e-06
LANES = 128
CHUNK = 64
SLOTS = WINDOW // UNIT
FAR = -1e30
SIDES = ("send", "keep")
VMEM_BYTES = 66_000_000
BF = jnp.bfloat16
F32 = jnp.float32
ROOT = math.sqrt(2.0 / math.pi)
CUBIC = 0.044715


def dot_nn(left, right):
    return jnp.dot(left, right, preferred_element_type=F32)


def dot_nt(left, right):
    return lax.dot_general(left, right, (((1,), (1,)), ((), ())), preferred_element_type=F32)


def dot_tn(left, right):
    return lax.dot_general(left, right, (((0,), (0,)), ((), ())), preferred_element_type=F32)


SMALL = pl.BlockSpec(memory_space=pltpu.SMEM)
NEAR = pl.BlockSpec(memory_space=pltpu.VMEM)
ANY = pl.BlockSpec(memory_space=pl.ANY)


class Work:
    def __init__(self, ins, outs, scratch, in_sems, out_sems):
        self.ins, self.outs, self.scratch, self.out_sems = ins, outs, scratch, out_sems
        self.copies, self.waited, self.flushed = {}, set(), []
        for index, (name, (ref, buffer)) in enumerate(ins.items()):
            self.copies[name] = pltpu.make_async_copy(ref, buffer, in_sems.at[index])
            self.copies[name].start()

    def __getattr__(self, name):
        if name in self.__dict__["ins"]:
            return self.ins[name][1]
        if name in self.__dict__["outs"]:
            return self.outs[name][1]
        return self.__dict__["scratch"][name]

    def has(self, name):
        return name in self.outs

    def takes(self, name):
        return name in self.ins

    def send(self, name, source, *at):
        ref = self.outs[name][0]
        copy = pltpu.make_async_copy(
            source, ref.at[at] if at else ref, self.out_sems.at[len(self.flushed)]
        )
        copy.start()
        self.flushed.append(copy)

    def need(self, *names):
        for name in names:
            if name not in self.waited:
                self.waited.add(name)
                self.copies[name].wait()

    def flush(self, name, *at):
        ref, buffer = self.outs[name]
        if at:
            ref, buffer = ref.at[at], buffer.at[at]
        copy = pltpu.make_async_copy(buffer, ref, self.out_sems.at[len(self.flushed)])
        copy.start()
        self.flushed.append(copy)

    def finish(self):
        self.need(*self.ins)
        for copy in self.flushed:
            copy.wait()


class Names:
    def __init__(self, work, **names):
        self.work, self.names = work, names

    def to(self, name):
        return self.__dict__["names"].get(name, name)

    def __getattr__(self, name):
        return getattr(self.__dict__["work"], self.to(name))

    @property
    def outs(self):
        return {name: self.work.outs[self.to(name)] for name in SIDES}

    def has(self, name):
        return self.work.has(self.to(name))

    def takes(self, name):
        return self.work.takes(self.to(name))

    def need(self, *names):
        self.work.need(*[name for name in map(self.to, names) if self.work.takes(name)])

    def flush(self, name, *at):
        if self.has(name):
            self.work.flush(self.to(name), *at)


def run(body, name, info, ins, small, weights, outs, small_outs, scratch, after=(), cost=1.0):
    in_names, out_names, names = list(ins), list(outs), list(scratch)
    small_names, small_out_names = list(small), list(small_outs)
    counts = [1, len(in_names), len(small), len(weights), len(after), len(outs), len(small_outs)]

    def kernel(*refs):
        refs = list(refs)
        parts = []
        for count in counts:
            parts.append(refs[:count])
            refs = refs[count:]
        (info_ref,), in_refs, small_refs, weight_refs, _, out_refs, small_out_refs = parts
        in_bufs, refs = refs[: len(in_names)], refs[len(in_names) :]
        out_bufs, refs = refs[: len(out_names)], refs[len(out_names) :]
        rest, (in_sems, out_sems) = refs[:-2], refs[-2:]
        extra = {}
        rest = list(rest)
        for key in names:
            many = isinstance(scratch[key], list)
            size = len(scratch[key]) if many else 1
            extra[key] = rest[:size] if many else rest[0]
            rest = rest[size:]
        for key, ref in zip(small_names, small_refs):
            index = small[key][1]
            extra[key] = ref.at[index] if index else ref
        extra.update(zip(small_out_names, small_out_refs))
        work = Work(
            dict(zip(in_names, zip(in_refs, in_bufs))),
            dict(zip(out_names, zip(out_refs, out_bufs))),
            extra,
            in_sems,
            out_sems,
        )
        body(info_ref, work, weight_refs)
        work.finish()

    buffer = lambda a: pltpu.VMEM(a.shape, a.dtype)
    flat = []
    for value in scratch.values():
        flat += value if isinstance(value, list) else [value]
    results = pl.pallas_call(
        kernel,
        out_shape=[outs[n] for n in out_names] + [small_outs[n] for n in small_out_names],
        in_specs=[SMALL]
        + [ANY] * len(ins)
        + [NEAR] * len(small)
        + [ANY] * (len(weights) + len(after)),
        out_specs=[ANY] * len(outs) + [NEAR] * len(small_outs),
        scratch_shapes=[buffer(ins[n]) for n in in_names]
        + [buffer(outs[n]) for n in out_names]
        + flat
        + [pltpu.SemaphoreType.DMA((max(len(ins), 1),)), pltpu.SemaphoreType.DMA((32,))],
        compiler_params=pltpu.CompilerParams(vmem_limit_bytes=VMEM_BYTES),
        cost_estimate=lasting(cost),
        name=name,
    )(info, *ins.values(), *[array for array, _ in small.values()], *weights, *after)
    return results


def plain(body, name, info, ins, outs, scratch=(), after=()):
    first = len(ins) + (0 if info is None else 1)
    results = pl.pallas_call(
        lambda *refs: body(*refs[:first], *refs[first + len(after) :]),
        out_shape=outs,
        in_specs=([] if info is None else [SMALL]) + [NEAR] * len(ins) + [ANY] * len(after),
        out_specs=[NEAR] * len(outs),
        scratch_shapes=list(scratch),
        compiler_params=pltpu.CompilerParams(vmem_limit_bytes=VMEM_BYTES),
        cost_estimate=lasting(0.05),
        name=name,
    )(*([] if info is None else [info]), *ins, *after)
    return results if len(outs) > 1 else results[0]


def lasting(units):
    return pl.CostEstimate(flops=int(units * 0.4e9), bytes_accessed=1000, transcendentals=0)


def shape(*dims, dtype=F32):
    return jax.ShapeDtypeStruct(dims, dtype)


def start_rows(refs, place, plan, sems):
    own, sib, xa, ya, xb, yb = refs
    half = own.shape[0] // 2
    for rank in range(4):
        for parity in range(2):

            @pl.when(place == rank * 2 + parity)
            def _(rank=rank, parity=parity):
                for index, (shard, row, rows, dst) in enumerate(plan):
                    step = shard ^ rank
                    if step < 2:
                        src = (own, sib)[step].at[pl.ds(row, rows)]
                    else:
                        first, second = ((xa, ya), (xb, yb))[step - 2]
                        part = row // half
                        src = (first if part == parity else second).at[pl.ds(row - part * half, rows)]
                    pltpu.make_async_copy(src, dst, sems.at[index]).start()


def wait_rows(refs, plan, sems, which):
    for index in which:
        _, row, rows, dst = plan[index]
        pltpu.make_async_copy(refs[0].at[pl.ds(0, rows)], dst, sems.at[index]).wait()


def plan_of(buffers, first, rows):
    return [
        (shard, (first + which) * rows, rows, dst.at[pl.ds(shard * rows, rows)])
        for which, dst in enumerate(buffers)
        for shard in range(4)
    ]


def norm_rows(values):
    mean = jnp.mean(values, axis=-1, keepdims=True)
    center = values - mean
    factor = lax.rsqrt(jnp.mean(center * center, axis=-1, keepdims=True) + EPSILON)
    return center * factor, factor


def piece(mod, slot, index):
    width = mod.shape[1] // 9
    return mod[pl.ds(slot, 1), index * width : (index + 1) * width]


def entry_rows(x, mod, info, index, out):
    for block in range(x.shape[0] // UNIT):
        slot = info[1 + block]
        shift = piece(mod, slot, index)
        scale = 1.0 + piece(mod, slot, index + 1)

        def step(turn, carry):
            rows = pl.ds(pl.multiple_of(block * UNIT + turn * CHUNK, CHUNK), CHUNK)
            normed, _ = norm_rows(x[rows, :])
            out[rows, :] = (normed * scale + shift).astype(BF)
            return carry

        lax.fori_loop(0, UNIT // CHUNK, step, 0, unroll=True)


def residual_rows(x, mod, info, index, branch, branch_out, out, low=None):
    for block in range(x.shape[0] // UNIT):
        gate = piece(mod, info[1 + block], index)

        def step(turn, carry):
            rows = pl.ds(pl.multiple_of(block * UNIT + turn * CHUNK, CHUNK), CHUNK)
            values = branch[rows, :]
            branch_out[rows, :] = values.astype(BF)
            result = x[rows, :] + gate * values
            out[rows, :] = result
            if low is not None:
                low[rows, :] = result.astype(BF)
            return carry

        lax.fori_loop(0, UNIT // CHUNK, step, 0, unroll=True)


def fold(values):
    return jnp.sum(values.reshape(values.shape[0] // 8, 8, values.shape[1]), axis=0)


def total(values):
    return jnp.sum(values, axis=0, keepdims=True)


def gate_back(g, mod, info, index, branch, gb, stats):
    width = g.shape[1]
    sums = jnp.zeros((8, width), F32)
    for block in range(g.shape[0] // UNIT):
        slot = info[1 + block]
        gate = piece(mod, slot, index)

        def step(turn, carry):
            rows = pl.ds(pl.multiple_of(block * UNIT + turn * CHUNK, CHUNK), CHUNK)
            grad = g[rows, :]
            low = (gate * grad).astype(BF)
            gb[rows, :] = low
            return (
                carry[0] + fold(low.astype(F32)),
                carry[1] + fold(grad * branch[rows, :].astype(F32)),
            )

        sums, rows_sum = lax.fori_loop(
            0, UNIT // CHUNK, step, (sums, jnp.zeros((8, width), F32)), unroll=True
        )
        stats[pl.ds(8 + slot, 1), :] += total(rows_sum)
    stats[12:13, :] = total(sums)


def norm_back_rows(x, g, de, mod, info, index, out, stats, low=None):
    width = x.shape[1]
    for block in range(x.shape[0] // UNIT):
        slot = info[1 + block]
        scale = 1.0 + piece(mod, slot, index + 1)

        def step(turn, carry):
            rows = pl.ds(pl.multiple_of(block * UNIT + turn * CHUNK, CHUNK), CHUNK)
            normed, factor = norm_rows(x[rows, :])
            grad = de[rows, :]
            inner = grad * normed
            dn = grad * scale
            mean = jnp.mean(dn, axis=-1, keepdims=True)
            along = jnp.mean(dn * normed, axis=-1, keepdims=True)
            result = g[rows, :] + factor * (dn - mean - normed * along)
            out[rows, :] = result
            if low is not None:
                low[rows, :] = result.astype(BF)
            return (carry[0] + fold(grad), carry[1] + fold(inner))

        zero = jnp.zeros((8, width), F32)
        shift_sum, scale_sum = lax.fori_loop(0, UNIT // CHUNK, step, (zero, zero), unroll=True)
        stats[pl.ds(slot, 1), :] += total(shift_sum)
        stats[pl.ds(4 + slot, 1), :] += total(scale_sum)


def lane_ids(rows):
    return lax.broadcasted_iota(jnp.int32, (rows, LANES), 1)


def head_half(values, half):
    ids = lane_ids(values.shape[0])
    keep = ids < HEAD_WIDTH if half == 0 else ids >= HEAD_WIDTH
    return jnp.where(keep, values.astype(F32), 0.0)


def turned_halves(keys):
    turned = keys.T
    low = lax.broadcasted_iota(jnp.int32, turned.shape, 0) < HEAD_WIDTH
    zero = jnp.zeros(turned.shape, turned.dtype)
    return jnp.concatenate([jnp.where(low, turned, zero), jnp.where(low, zero, turned)], axis=1)


def query_marks(slot):
    return jnp.where(lane_ids(UNIT) == slot, 1.0, 0.0).astype(BF)


def key_marks(slots):
    ids = lane_ids(UNIT)
    parts = [jnp.where((ids < SLOTS) & (ids != slot), FAR, 0.0).astype(BF) for slot in slots]
    return jnp.concatenate(parts, axis=0)


def pair_lanes(pair):
    return pl.ds(pl.multiple_of(pair * LANES, LANES), LANES)


def start_own_rows(info, work, whole):
    share = work.rows.shape[0]
    first = pl.multiple_of((info[5] % 2) * share, share)
    copy = pltpu.make_async_copy(whole.at[pl.ds(first, share)], work.rows, work.row_sems.at[0])
    copy.start()
    return copy


def raise_rows(low, out):
    for row in range(0, low.shape[0], CHUNK):
        span = pl.ds(row, CHUNK)
        out[span, :] = low[span, :].astype(F32)


def kv_kernel(info, work, weights):
    rows = weights[0].shape[0] // 4
    plan = plan_of((work.w.at[0], work.w.at[1]), 1, rows)
    start_rows(weights[:6], info[0], plan, work.sems)
    if work.has("branch"):
        work.need("part", "other", "below")
        bias = work.bias[...].astype(F32)
        for row in range(0, work.sum.shape[0], CHUNK):
            span = pl.ds(row, CHUNK)
            work.sum[span, :] = (
                work.part[span, :].astype(F32) + work.other[span, :].astype(F32) + bias
            )
        residual_rows(work.below, work.mod_below, info, 8, work.sum, work.branch, work.x)
        work.flush("branch")
        work.flush("x")
    else:
        start_own_rows(info, work, weights[6]).wait()
        raise_rows(work.rows, work.x)
        work.flush("x")
    entry_rows(work.x, work.mod, info, 0, work.entry)
    work.flush("entry")
    entry = work.entry[...]
    wait_rows(weights, plan, work.sems, range(4))
    work.kv[0] = dot_nt(entry, work.w[0]).astype(BF)
    work.flush("kv", 0)
    wait_rows(weights, plan, work.sems, range(4, 8))
    work.kv[1] = (dot_nt(entry, work.w[1]) + work.biases[2:3, :]).astype(BF)
    work.flush("kv", 1)


def q_kernel(info, work, weights):
    rows = weights[0].shape[0] // 4
    plan = plan_of((work.w,), 0, rows)
    start_rows(weights, info[0], plan, work.sems)
    work.need("entry")
    wait_rows(weights, plan, work.sems, range(4))
    work.q[...] = (dot_nt(work.entry[...], work.w[...]) + work.biases[0:1, :]).astype(BF)
    work.flush("q")


def soft_pair(work, q_pair, keys, values, marks, logs, pair, span, words=None):
    ids = lane_ids(UNIT)
    results = []
    kept = logs[span, :]
    for half in range(2):
        left = (head_half(q_pair, half) * HEAD_WIDTH**-0.5).astype(BF)
        if marks is not None:
            left = jnp.concatenate([left, marks], axis=1)
        scores = dot_nt(left, keys)
        if words is not None:
            scores = jnp.where(ids < words, scores, FAR)
        peak = jnp.max(scores, axis=-1, keepdims=True)
        both = dot_nn(jnp.exp(scores - peak).astype(BF), values)
        sums = both[:, LANES:]
        results.append(both[:, :LANES] / sums)
        kept = jnp.where(ids == 2 * pair + half, peak + jnp.log(sums), kept)
    logs[span, :] = kept
    return jnp.where(ids < HEAD_WIDTH, results[0], results[1])


def self_kernel(info, work, weights):
    rows = weights[0].shape[0] // 4
    sems = work.sems
    plan = [(s, 3 * rows, rows, work.wo.at[pl.ds(s * rows, rows)]) for s in range(4)]
    start_rows(weights, info[0], plan, sems)
    share = work.x.shape[0]
    blocks = share // UNIT
    marks = key_marks([info[1 + b] for b in range(2 * blocks)])
    ones = jnp.ones((2 * share, LANES), BF)
    logs, mixed = work.logs, work.mixed
    logs[...] = jnp.zeros(logs.shape, F32)
    work.need("q", "kv_own", "kv_sib")

    def both(which, lanes):
        return jnp.concatenate([work.kv_own[which, :, lanes], work.kv_sib[which, :, lanes]], axis=0)

    def step(pair, carry):
        lanes = pair_lanes(pair)
        keys = jnp.concatenate([both(0, lanes), marks], axis=1)
        values = jnp.concatenate([both(1, lanes), ones], axis=1)
        for block in range(blocks):
            span = pl.ds(block * UNIT, UNIT)
            values_mixed = soft_pair(
                work,
                work.q[span, lanes],
                keys,
                values,
                query_marks(info[1 + block]),
                logs,
                pair,
                span,
            )
            low = values_mixed.astype(BF)
            mixed[span, lanes] = low
            work.rest[span, lanes] = (values_mixed - low.astype(F32)).astype(BF)
        return carry

    lax.fori_loop(0, mixed.shape[1] // LANES, step, 0)
    work.flush("mixed")
    work.flush("rest")
    work.lse[...] = logs[...].T[: work.lse.shape[0], :]
    work.flush("lse")
    wait_rows(weights, plan, sems, range(4))
    work.sum[...] = dot_nn(mixed[...], work.wo[...]) + work.bias[...].astype(F32)
    work.need("x")
    residual_rows(work.x, work.mod, info, 2, work.sum, work.branch, work.out)
    work.flush("branch")
    work.flush("out")


def cross_kernel(info, work, weights, words):
    rows = weights[0].shape[0] // 4
    sems = work.sems
    order = (1, 2, 0, 3)
    plan = [
        (shard, order[i // 4] * rows, count, dst)
        for i, (shard, _, count, dst) in enumerate(
            plan_of((work.wk, work.wv, work.wq, work.wo), 0, rows)
        )
    ]
    start_rows(weights, info[0], plan, sems)
    work.need("x")
    entry_rows(work.x, work.mod, info, 3, work.entry)
    work.flush("entry")
    work.need("text")
    wait_rows(weights, plan, sems, range(0, 4))
    work.kv[0] = dot_nt(work.text[...], work.wk[...]).astype(BF)
    wait_rows(weights, plan, sems, range(4, 8))
    work.kv[1] = (dot_nt(work.text[...], work.wv[...]) + work.biases[5:6, :]).astype(BF)
    work.flush("kv")
    wait_rows(weights, plan, sems, range(8, 12))
    work.q[...] = (dot_nt(work.entry[...], work.wq[...]) + work.biases[3:4, :]).astype(BF)
    work.flush("q")
    ones = jnp.ones((LANES, LANES), BF)
    logs, mixed = work.logs, work.mixed
    logs[...] = jnp.zeros(logs.shape, F32)

    def step(pair, carry):
        lanes = pair_lanes(pair)
        for block in range(mixed.shape[0] // UNIT):
            span = pl.ds(block * UNIT, UNIT)
            own = pl.ds(pl.multiple_of(info[1 + block] * LANES, LANES), LANES)
            mixed[span, lanes] = soft_pair(
                work,
                work.q[span, lanes],
                work.kv[0, own, lanes],
                jnp.concatenate([work.kv[1, own, lanes], ones], axis=1),
                None,
                logs,
                pair,
                span,
                words,
            ).astype(BF)
        return carry

    lax.fori_loop(0, mixed.shape[1] // LANES, step, 0, unroll=2)
    work.flush("mixed")
    work.lse[...] = logs[...].T[: work.lse.shape[0], :]
    work.flush("lse")
    wait_rows(weights, plan, sems, range(12, 16))
    work.sum[...] = dot_nn(mixed[...], work.wo[...]) + work.bias[...].astype(F32)
    residual_rows(work.x, work.mod, info, 5, work.sum, work.branch, work.out)
    work.flush("branch")
    work.flush("out")


def hidden_plan(refs, buffer):
    rows = buffer.shape[1]
    half = rows // 2
    return [
        (shard, row, half, buffer.at[shard, pl.ds(row, half)])
        for shard in range(4)
        for row in range(0, rows, half)
    ]


def start_chip(info, refs, layer, buffer, sems):
    copies = [
        pltpu.make_async_copy(ref.at[layer], buffer.at[(info[5] + i) % 2], sems.at[i])
        for i, ref in enumerate(refs)
    ]
    for copy in copies:
        copy.start()
    return copies


def bend_rows(before, bias, active, slope, lanes):
    for row in range(0, before.shape[0], CHUNK):
        span = pl.ds(row, CHUNK)
        values = before[span, :] + bias
        square = values * values
        half = 1.0 / (1.0 + jnp.exp(values * (-2.0 * ROOT - (2.0 * ROOT * CUBIC) * square)))
        act = values * half
        active[span, lanes] = act.astype(BF)
        slope[span, lanes] = (
            half + act * (1.0 - half) * (2.0 * ROOT + (6.0 * ROOT * CUBIC) * square)
        ).astype(BF)


def columns_of(shard, width):
    return pl.ds(pl.multiple_of(shard * width, width), width)


def start_hidden(info, work, weights, layer):
    if len(weights) == 4:
        ups = start_chip(info, weights[:2], layer, work.up, work.sems)
        downs = start_chip(info, weights[2:], layer, work.down, work.down_sems)
        return [lambda some=some: [copy.wait() for copy in some] for some in (ups, downs)]
    waits = []
    for refs, buffer, sems in (
        (weights[:6], work.up, work.sems),
        (weights[6:12], work.down, work.down_sems),
    ):
        refs = [ref.at[layer] for ref in refs[:2]] + list(refs[2:])
        plan = hidden_plan(refs, buffer)
        start_rows(refs, info[0], plan, sems)
        waits.append(
            lambda refs=refs, plan=plan, sems=sems: wait_rows(refs, plan, sems, range(len(plan)))
        )
    return waits


def hidden_kernel(info, work, weights, layer):
    waits = start_hidden(info, work, weights, layer)
    width = work.x.shape[1]
    shards = work.up.shape[0]
    first = info[6] * 2
    work.need("x")
    entry_rows(work.x, work.mod, info, 6, work.entry)
    work.flush("entry")
    for wait in waits:
        wait()
    work.sum[...] = jnp.zeros(work.sum.shape, F32)

    def step(shard, carry):
        lanes = columns_of(shard, width)
        bias = work.up_bias[:, columns_of(first + shard, width)]
        work.before[...] = dot_nn(work.entry[...], work.up[shard])
        bend_rows(work.before, bias, work.active, work.slope, lanes)
        work.sum[...] += dot_nn(work.active[:, lanes], work.down[shard])
        return carry

    lax.fori_loop(0, shards, step, 0)
    work.flush("active")
    work.flush("slope")
    work.part[...] = work.sum[...].astype(BF)
    work.flush("part")


def hidden_back_kernel(info, work, weights, layer):
    waits = start_hidden(info, work, weights, layer)
    work.stats[...] = jnp.zeros(work.stats.shape, F32)
    stats = work.stats.at[pl.ds(48, 24)]
    work.need("g", "branch")
    gate_back(work.g, work.mod, info, 8, work.branch, work.gb, stats)
    work.need("slope")
    for wait in waits:
        wait()
    hidden_back_rows(info, work, work.de, stats)
    work.part[...] = work.de[...].astype(BF)
    work.flush("part")
    work.flush("gb")
    work.flush("d_before")


def hidden_back_rows(info, work, de, stats):
    width = work.g.shape[1]
    shards = work.up.shape[0]
    first = info[6] * 2 if shards == 2 else 0
    de[...] = jnp.zeros(de.shape, F32)

    def step(shard, carry):
        lanes = columns_of(shard, width)
        work.before[...] = dot_nt(work.gb[...], work.down[shard])
        sums = jnp.zeros((8, width), F32)
        for row in range(0, work.g.shape[0], CHUNK):
            span = pl.ds(row, CHUNK)
            low = (work.before[span, :] * work.slope[span, lanes].astype(F32)).astype(BF)
            work.d_before[span, lanes] = low
            sums += fold(low.astype(F32))
        stats[pl.ds(13 + first + shard, 1), :] = total(sums)
        de[...] += dot_nt(work.d_before[:, lanes], work.up[shard])
        return carry

    lax.fori_loop(0, shards, step, 0)


def hidden_both_kernel(info, work, weights, layer):
    copy = start_own_rows(info, work, weights[12])
    waits = start_hidden(info, work, weights, layer)
    width = work.x.shape[1]
    work.need("x")
    entry_rows(work.x, work.mod, info, 6, work.entry)
    for wait in waits:
        wait()
    work.sum[...] = jnp.zeros(work.sum.shape, F32) + work.bias[...].astype(F32)

    def step(shard, carry):
        lanes = columns_of(shard, width)
        work.before[...] = dot_nn(work.entry[...], work.up[shard])
        bend_rows(work.before, work.up_bias[:, lanes], work.active, work.slope, lanes)
        work.sum[...] += dot_nn(work.active[:, lanes], work.down[shard])
        return carry

    lax.fori_loop(0, 4, step, 0)
    residual_rows(work.x, work.mod, info, 8, work.sum, work.branch, work.out, work.low)
    work.flush("low")
    work.stats[...] = jnp.zeros(work.stats.shape, F32)
    stats = work.stats.at[pl.ds(48, 24)]
    copy.wait()
    raise_rows(work.rows, work.g)
    gate_back(work.g, work.mod, info, 8, work.branch, work.gb, stats)
    hidden_back_rows(info, work, work.sum, stats)
    left, right = work.entry[...].T, work.gb[...].T
    for name, rank in zip(SIDES, (info[7], info[5])):
        out = work.outs[name][1]
        lanes = columns_of(rank, width)
        out[:, :width] = dot_nn(left, work.d_before[:, lanes]).astype(BF)
        out[:, width:] = dot_nn(right, work.active[:, lanes]).astype(BF)
        work.flush(name)
    norm_back_rows(work.x, work.g, work.sum, work.mod, info, 6, work.out, stats)
    work.flush("out")


def hidden_cross_kernel(info, work, weights, words):
    hidden_both_kernel(
        info,
        Names(
            work,
            x="x2",
            entry="entry3",
            branch="branch3",
            out="g_mid",
            send="f_send",
            keep="f_keep",
        ),
        weights[:13],
        1,
    )
    cross_back_kernel(
        info,
        Names(
            work,
            early="stats",
            g="g_mid",
            branch="branch2",
            entry="entry2",
            x="x1",
            de="sum",
            dq="entry3",
            d_mixed="rows",
            sems="csems",
            send="c_send",
            keep="c_keep",
        ),
        weights[13:],
        words,
    )


def attention_kernel(info, work, weights, words):
    self_kernel(
        info,
        Names(work, out="x1", mixed="mixed1", lse="lse1", branch="branch1", bias="self_bias"),
        weights[:6],
    )
    cross_kernel(
        info,
        Names(
            work,
            x="x1",
            q="cq",
            kv="ckv",
            mixed="mixed2",
            lse="lse2",
            branch="branch2",
            bias="cross_bias",
            wo="cross_wo",
            sems="csems",
        ),
        weights[6:],
        words,
    )


def hidden_grads_kernel(info, work, weights):
    width = work.entry.shape[1]
    work.need("entry", "d_before", "gb", "active")
    left, right = work.entry[...].T, work.gb[...].T
    for name, shift in zip(SIDES, (1, 0)):
        out = work.outs[name][1]
        lanes = columns_of((info[5] + shift) % 2, width)
        out[:, :width] = dot_nn(left, work.d_before[:, lanes]).astype(BF)
        out[:, width:] = dot_nn(right, work.active[:, lanes]).astype(BF)
        work.flush(name)


def pair_grads(info, work, members):
    rows = members[0][0].shape[0]
    low = lane_ids(rows) < HEAD_WIDTH
    step = 3 * LANES
    for at in range(len(members) // 2):
        products = [dot_nn(left, right) for left, right in members[2 * at : 2 * at + 2]]
        (a0, a1, a2), (b0, b1, b2) = [
            [p[:, i * LANES : (i + 1) * LANES] for i in range(3)] for p in products
        ]
        even = (a0, b0, jnp.where(low, a1, pltpu.roll(b1, HEAD_WIDTH, 1)))
        a1, b1 = pltpu.roll(a1, HEAD_WIDTH, 1), pltpu.roll(b1, HEAD_WIDTH, 1)
        a2r, b2r = pltpu.roll(a2, HEAD_WIDTH, 1), pltpu.roll(b2, HEAD_WIDTH, 1)
        odd = (jnp.where(low, a1, a2r), jnp.where(low, b1, b2r), jnp.where(low, a2r, b2))
        first = info[5] % 2 == 0
        for i, (mine, other) in enumerate(zip(even, odd)):
            lanes = pl.ds(at * step + i * LANES, LANES)
            work.outs["keep"][1][:, lanes] = jnp.where(first, mine, other).astype(BF)
            work.outs["send"][1][:, lanes] = jnp.where(first, other, mine).astype(BF)
    work.flush("send")
    work.flush("keep")


def chip_lanes(info, width):
    return pl.ds(pl.multiple_of(info[6] * (width // 2), width // 2), width // 2)


def query_output_kernel(info, work, weights):
    work.need("entry", "gb", "dq", "mixed")
    lanes = chip_lanes(info, work.dq.shape[1])
    pair_grads(
        info,
        work,
        [
            (work.entry[...].T, work.dq[:, lanes]),
            (work.gb[...].T, work.mixed[:, lanes]),
        ],
    )


def cross_back_kernel(info, work, weights, words):
    rows = weights[0].shape[0] // 4
    sems = work.sems
    plan = [
        (shard, (3 * rows, 0)[i // 4], count, dst)
        for i, (shard, _, count, dst) in enumerate(plan_of((work.wo, work.wq), 0, rows))
    ]
    start_rows(weights, info[0], plan, sems)
    work.stats[...] = work.early[...]
    stats = work.stats.at[pl.ds(24, 24)]
    g = work.g
    work.need("g")
    if work.takes("part"):
        work.need("part", "other", "above")
        for row in range(0, g.shape[0], CHUNK):
            span = pl.ds(row, CHUNK)
            work.de[span, :] = work.part[span, :].astype(F32) + work.other[span, :].astype(F32)
        g = work.g_mid
        norm_back_rows(
            work.above, work.g, work.de, work.mod, info, 6, g, work.stats.at[pl.ds(48, 24)]
        )
    work.need("branch")
    gate_back(g, work.mod, info, 5, work.branch, work.gb, stats)
    wait_rows(weights, plan, sems, range(0, 4))
    work.d_mixed[...] = dot_nt(work.gb[...], work.wo[...]).astype(BF)
    work.dkv_sum[...] = jnp.zeros(work.dkv_sum.shape, F32)
    real = lax.broadcasted_iota(jnp.int32, (LANES, UNIT), 0) < words
    work.need("q", "kv", "lse")

    def step(pair, carry):
        lanes = pair_lanes(pair)
        for block in range(work.q.shape[0] // UNIT):
            span = pl.ds(block * UNIT, UNIT)
            own = pl.ds(pl.multiple_of(info[1 + block] * LANES, LANES), LANES)
            q_pair = work.q[span, lanes]
            d_pair = work.d_mixed[span, lanes]
            keys = work.kv[0, own, lanes]
            values = work.kv[1, own, lanes]
            lefts, grads, probs_low, scores_low = [], [], [], []
            for half in range(2):
                left = (head_half(q_pair, half) * HEAD_WIDTH**-0.5).astype(BF)
                grad = head_half(d_pair, half).astype(BF)
                logs = work.lse[pl.ds(2 * pair + half, 1), span]
                probs = jnp.where(real, jnp.exp(dot_nt(keys, left) - logs), 0.0)
                d_probs = dot_nt(values, grad)
                inner = jnp.sum(probs * d_probs, axis=0, keepdims=True)
                lefts.append(left)
                grads.append(grad)
                probs_low.append(probs.astype(BF))
                scores_low.append((probs * (d_probs - inner)).astype(BF))
            wide_scores = jnp.concatenate(scores_low, axis=1)
            grad_v = dot_nn(jnp.concatenate(probs_low, axis=1), jnp.concatenate(grads, axis=0))
            grad_k = dot_nn(wide_scores, jnp.concatenate(lefts, axis=0))
            grad_q = dot_nn(turned_halves(keys), jnp.concatenate(scores_low, axis=0))
            work.dq[span, lanes] = (grad_q.T * HEAD_WIDTH**-0.5).astype(BF)
            work.dkv_sum[0, own, lanes] += grad_k
            work.dkv_sum[1, own, lanes] += grad_v
        return carry

    lax.fori_loop(0, work.q.shape[1] // LANES, step, 0, unroll=2)
    work.dkv[...] = work.dkv_sum[...].astype(BF)
    work.need("entry", "text", "mixed")
    lanes = chip_lanes(info, work.dq.shape[1])
    text = work.text[...].T
    pair_grads(
        info,
        work,
        [
            (work.entry[...].T, work.dq[:, lanes]),
            (text, work.dkv[0, :, lanes]),
            (text, work.dkv[1, :, lanes]),
            (work.gb[...].T, work.mixed[:, lanes]),
        ],
    )
    stats[13:14, :] = total(fold(work.dq[...].astype(F32)))
    stats[14:15, :] = total(fold(work.dkv[1].astype(F32)))
    wait_rows(weights, plan, sems, range(4, 8))
    work.de[...] = dot_nn(work.dq[...], work.wq[...])
    work.need("x")
    norm_back_rows(work.x, g, work.de, work.mod, info, 3, work.out, stats)
    work.flush("out")


def self_back_kernel(info, work, weights):
    rows = weights[0].shape[0] // 4
    sems = work.sems
    plan = [(s, 3 * rows, rows, work.wo.at[pl.ds(s * rows, rows)]) for s in range(4)]
    start_rows(weights, info[0], plan, sems)
    work.stats[...] = work.early[...]
    stats = work.stats.at[pl.ds(0, 24)]
    work.need("g", "branch")
    gate_back(work.g, work.mod, info, 2, work.branch, work.gb, stats)
    work.flush("gb")
    share = work.g.shape[0]
    blocks = share // UNIT
    marks = key_marks([info[1 + b] for b in range(2 * blocks)])
    wait_rows(weights, plan, sems, range(4))
    work.d_mixed[...] = dot_nt(work.gb[...], work.wo[...]).astype(BF)
    work.need("mixed", "rest", "q", "kv_own", "kv_sib", "lse")
    width = work.q.shape[1]
    head = lax.broadcasted_iota(jnp.int32, (16, width), 0)
    lane = lax.broadcasted_iota(jnp.int32, (16, width), 1)
    first = head * HEAD_WIDTH
    pick = jnp.where((lane >= first) & (lane < first + HEAD_WIDTH), 1.0, 0.0)
    for block in range(blocks):
        span = pl.ds(block * UNIT, UNIT)
        whole = work.mixed[span, :].astype(F32) + work.rest[span, :].astype(F32)
        work.inner[:, span] = lax.dot_general(
            pick,
            whole * work.d_mixed[span, :].astype(F32),
            (((1,), (1,)), ((), ())),
            precision=lax.Precision.HIGHEST,
            preferred_element_type=F32,
        )

    def both(which, lanes):
        return jnp.concatenate([work.kv_own[which, :, lanes], work.kv_sib[which, :, lanes]], axis=0)

    def step(pair, carry):
        lanes = pair_lanes(pair)
        keys = both(0, lanes)
        values = both(1, lanes)
        marked = jnp.concatenate([keys, marks], axis=1)
        turned = turned_halves(keys)
        lefts, grads, probs_low, scores_low = [], [], [], []
        for block in range(blocks):
            span = pl.ds(block * UNIT, UNIT)
            q_pair = work.q[span, lanes]
            d_pair = work.d_mixed[span, lanes]
            ends = query_marks(info[1 + block])
            for half in range(2):
                left = (head_half(q_pair, half) * HEAD_WIDTH**-0.5).astype(BF)
                grad = head_half(d_pair, half).astype(BF)
                logs = work.lse[pl.ds(2 * pair + half, 1), span]
                probs = jnp.exp(dot_nt(marked, jnp.concatenate([left, ends], axis=1)) - logs)
                d_probs = dot_nt(values, grad)
                inner = work.inner[pl.ds(2 * pair + half, 1), span]
                lefts.append(left)
                grads.append(grad)
                probs_low.append(probs.astype(BF))
                scores_low.append((probs * (d_probs - inner)).astype(BF))
            grad_q = dot_nn(turned, jnp.concatenate(scores_low[-2:], axis=0))
            work.dq[span, lanes] = (grad_q.T * HEAD_WIDTH**-0.5).astype(BF)
        grad_v = dot_nn(jnp.concatenate(probs_low, axis=1), jnp.concatenate(grads, axis=0))
        grad_k = dot_nn(jnp.concatenate(scores_low, axis=1), jnp.concatenate(lefts, axis=0))
        for which, grad in ((0, grad_k.astype(BF)), (1, grad_v.astype(BF))):
            work.dkv_own[which, :, lanes] = grad[:share]
            work.dkv_give[which, :, lanes] = grad[share:]
        return carry

    lax.fori_loop(0, work.q.shape[1] // LANES, step, 0)
    work.flush("dkv_give")
    work.flush("dkv_own")
    work.flush("dq")


def sum_keys_values(info, work, dkv):
    work.need("dkv_own", "dkv_sib")
    for which in range(2):
        dkv[which] = (
            work.dkv_own[which].astype(F32) + work.dkv_sib[which].astype(F32)
        ).astype(BF)
    work.need("entry")
    lanes = chip_lanes(info, dkv.shape[2])
    entry = work.entry[...].T
    pair_grads(info, work, [(entry, dkv[0, :, lanes]), (entry, dkv[1, :, lanes])])


def kv_grads_kernel(info, work, weights):
    sum_keys_values(info, work, work.dkv)
    work.flush("dkv")


def qkv_back_kernel(info, work, weights):
    rows = weights[0].shape[0] // 4
    sems = work.sems
    plan = plan_of((work.wq, work.wk, work.wv), 0, rows)
    start_rows(weights, info[0], plan, sems)
    work.stats[...] = work.early[...]
    stats = work.stats.at[pl.ds(0, 24)]
    if work.has("send"):
        sum_keys_values(info, work, work.dkv)
    else:
        work.need("dkv")
    work.need("dq")
    stats[13:14, :] = total(fold(work.dq[...].astype(F32)))
    stats[14:15, :] = total(fold(work.dkv[1].astype(F32)))
    wait_rows(weights, plan, sems, range(0, 12))
    work.de[...] = (
        dot_nn(work.dq[...], work.wq[...])
        + dot_nn(work.dkv[0], work.wk[...])
        + dot_nn(work.dkv[1], work.wv[...])
    )
    work.need("x", "g")
    low = work.low if work.has("low") else None
    norm_back_rows(work.x, work.g, work.de, work.mod, info, 0, work.out, stats, low)
    work.flush("out")
    if low is not None:
        work.flush("low")


def merge_kernel(info, *refs, spots, after):
    chains = len(spots)
    ins, outs = refs[: 4 * chains], refs[4 * chains + after :]
    for chain, (result, column) in enumerate(spots):
        for side in range(2):
            received, kept = ins[4 * chain + 2 * side], ins[4 * chain + 2 * side + 1]
            out = outs[2 * result + side]
            lanes = pl.ds(column, received.shape[2])
            out[:, :, lanes] = (received[...].astype(F32) + kept[...].astype(F32)).astype(BF)


def gate(arrays, after):
    count = len(arrays)
    return pl.pallas_call(
        lambda *refs: None,
        out_shape=[shape(*a.shape, dtype=a.dtype) for a in arrays],
        in_specs=[ANY] * (count + len(after)),
        out_specs=[ANY] * count,
        input_output_aliases={i: i for i in range(count)},
        cost_estimate=lasting(0.5),
        name="gate",
    )(*arrays, *after)


def pack_kernel(info, *refs, groups, whole, after):
    count = sum(len(members) for _, members in groups)
    sources, rest = refs[:count], refs[count + after :]
    (in_sems, out_sems), rest = rest[-2:], rest[:-2]
    count = len(groups) + sum(whole)
    outs, held = list(rest[:count]), rest[count:]
    owns = [outs.pop(0) if one else None for one in whole]
    spots = []
    at = 0
    for index, (layer, members) in enumerate(groups):
        rows = held[index].shape[0]
        piece_rows = rows // 4
        for quarter in range(4):
            row = quarter * piece_rows
            source = sources[at + quarter * len(members) // 4]
            src = source.at[layer, pl.ds(row % source.shape[1], piece_rows)]
            spots.append((index, quarter, held[index].at[pl.ds(row, piece_rows)], src))
        at += len(members)

    def arriving(place):
        _, _, spot, src = spots[place]
        return pltpu.make_async_copy(src, spot, in_sems.at[place])

    def leaving(index, which):
        if which == 2:
            return pltpu.make_async_copy(held[index], owns[index], out_sems.at[2 * index])
        rows = outs[index].shape[0]
        src = held[index].at[pl.ds(which * rows, rows)]
        return pltpu.make_async_copy(src, outs[index], out_sems.at[2 * index + 1])

    def by_parity(act):
        for parity in range(2):

            @pl.when(info[0] % 2 == parity)
            def _(parity=parity):
                act(parity)

    for place in range(len(spots)):
        arriving(place).start()
    for index in range(len(groups)):
        for quarter in range(4):
            arriving(4 * index + quarter).wait()
        by_parity(lambda parity: leaving(index, parity).start())
        if whole[index]:
            leaving(index, 2).start()
    for index in range(len(groups)):
        by_parity(lambda parity: leaving(index, parity).wait())
        if whole[index]:
            leaving(index, 2).wait()


def mod_kernel(condition, mod, mod_bias, q, v, cq, cv, up, out):
    narrow, units, columns = q.shape[1], up.shape[1], mod.shape[1]
    out[...] = jnp.zeros(out.shape, F32)
    for layer in range(LAYERS):
        row = pl.ds(layer, 1)
        out[layer, 0:SLOTS, 0:columns] = dot_nt(condition[...], mod[layer]) + mod_bias[
            row, :
        ].astype(F32)
        out[layer, 4:5, 0:units] = up[row, :].astype(F32)
        out[layer, 5:6, 0:narrow] = q[row, :].astype(F32)
        out[layer, 6:7, 0:narrow] = v[row, :].astype(F32)
        out[layer, 7:8, 0:narrow] = cq[row, :].astype(F32)
        out[layer, 4:5, 1024 : 1024 + narrow] = cv[row, :].astype(F32)


def assemble_kernel(info, *refs, narrow, units, columns):
    parts, (mods, narrows, ups) = refs[:4], refs[4:]
    narrows[...] = jnp.zeros(narrows.shape, F32)
    for rank in range(4):

        @pl.when(info[5] == rank)
        def _(rank=rank):
            for shard in range(4):
                part = parts[shard ^ rank]
                for layer in range(LAYERS):
                    mods[layer, :, shard * columns : (shard + 1) * columns] = part[
                        layer, 0:SLOTS, 0:columns
                    ]
                    ups[layer, :, shard * units : (shard + 1) * units] = part[layer, 4:5, 0:units]
                    at = slice(shard * narrow, (shard + 1) * narrow)
                    for row, source in ((0, 5), (2, 6), (3, 7)):
                        narrows[layer, row : row + 1, at] = part[
                            layer, source : source + 1, 0:narrow
                        ]
                    narrows[layer, 5:6, at] = part[layer, 4:5, 1024 : 1024 + narrow]


def collect_kernel(info, *refs, narrow, units, columns):
    stats, condition, out = refs[: 2 * LAYERS], refs[2 * LAYERS], refs[2 * LAYERS + 1]
    sums = refs[2 * LAYERS + 2]
    width = stats[0].shape[1]
    work = out
    out = refs[2 * LAYERS + 3]
    out[...] = jnp.zeros(out.shape, F32)
    for layer in range(LAYERS):
        sums[...] = stats[2 * layer][...] + stats[2 * layer + 1][...]
        base = 8 * layer
        out[base + 4 : base + 5, width : 2 * width] = sums[60:61, :]
        out[base + 5 : base + 6, 0:width] = sums[12:13, :]
        out[base + 5 : base + 6, width : 2 * width] = sums[36:37, :]
        for index in range(2):
            out[base + 6 + index : base + 7 + index, 512 : 512 + width] = condition[
                2 * layer + index : 2 * layer + index + 1, :
            ].astype(F32)
        for rank in range(4):

            @pl.when(info[5] == rank)
            def _(rank=rank, base=base):
                first = rank * columns
                for index in range(9):
                    low = max(first, index * width)
                    high = min(first + columns, (index + 1) * width)
                    if low < high:
                        row = (index // 3) * 24 + (index % 3) * 4
                        out[base : base + 4, low - first : high - first] = sums[
                            row : row + 4, low - index * width : high - index * width
                        ]
                out[base + 4 : base + 5, 0:units] = sums[61 + rank : 62 + rank, :]
                own = slice(rank * narrow, (rank + 1) * narrow)
                out[base + 6 : base + 7, 0:narrow] = sums[13:14, own]
                out[base + 6 : base + 7, 256 : 256 + narrow] = sums[14:15, own]
                out[base + 7 : base + 8, 0:narrow] = sums[37:38, own]
                out[base + 7 : base + 8, 256 : 256 + narrow] = sums[38:39, own]
    work[...] = out[...].astype(BF)


def spread_kernel(info, gathered, grad, bias_grad, q, v, cq, cv, up, o1, o2, o3, rows, conditions):
    count = gathered.shape[0]
    columns, part = grad.shape[2], grad.shape[1]
    width, narrow, units = conditions.shape[1], q.shape[1], up.shape[1]
    shift = lax.rem(width - info[8] * part, width)
    for index in range(count):
        for slot in range(SLOTS):
            row = 8 * (slot // 2) + 6 + slot % 2
            conditions[SLOTS * index + slot : SLOTS * index + slot + 1, :] = gathered[
                index ^ info[8], row : row + 1, 512 : 512 + width
            ].astype(F32)
    turned = pltpu.roll(conditions[...], shift, 1)[:, :part].T
    for layer in range(LAYERS):
        base = 8 * layer
        sums = jnp.zeros((8, gathered.shape[2]), F32)
        for index in range(count):
            values = gathered[index ^ info[8]].astype(F32)[base : base + 8]
            sums += values
            rows[SLOTS * index : SLOTS * (index + 1), :] = values[0:SLOTS, 0:columns]
        grad[layer] = jnp.dot(
            turned, rows[...], precision=lax.Precision.HIGHEST, preferred_element_type=F32
        )
        at = slice(layer, layer + 1)
        bias_grad[at, :] = jnp.sum(sums[0:SLOTS, 0:columns], axis=0, keepdims=True)
        up[at, :] = sums[4:5, 0:units]
        q[at, :] = sums[6:7, 0:narrow]
        v[at, :] = sums[6:7, 256 : 256 + narrow]
        cq[at, :] = sums[7:8, 0:narrow]
        cv[at, :] = sums[7:8, 256 : 256 + narrow]
        for out, row, lane in ((o1, 5, 0), (o2, 5, width), (o3, 4, width)):
            own = jnp.broadcast_to(sums[row : row + 1, lane : lane + width], (8, width))
            out[at, :] = pltpu.roll(own, shift, 1)[0:1, :part]


def finish_kernel(*refs, wide, spots):
    parts, outs = refs[: 2 * len(spots)], refs[2 * len(spots) :]
    step = 3 * LANES
    for chain, (at, places) in enumerate(spots):
        values = parts[2 * chain][0].astype(F32) + parts[2 * chain + 1][0].astype(F32)
        for layer, pair in places:
            if wide:
                width = outs[0].shape[2]
                for out in outs:
                    out[layer] = values[:, at : at + width]
                    at += width
                continue
            both = values[:, at : at + step]
            at += step
            first = jnp.concatenate(
                [both[:, :LANES], both[:, 2 * LANES : 2 * LANES + HEAD_WIDTH]], axis=1
            )
            second = jnp.concatenate(
                [both[:, LANES : 2 * LANES], both[:, 2 * LANES + HEAD_WIDTH :]], axis=1
            )
            for out, matrix in zip(outs[2 * pair : 2 * pair + 2], (first, second)):
                out[layer] = matrix if out.shape[1:] == matrix.shape else matrix.T


def join_kernel(info, rows, other, out):
    share = rows.shape[0]
    for core in range(2):

        @pl.when(info[5] % 2 == core)
        def _(core=core):
            out[pl.ds(core * share, share), :] = rows[...]
            out[pl.ds((1 - core) * share, share), :] = other[...]


def tensor_hop(values, step):
    return lax.ppermute(values, "tensor", [(i, i ^ step) for i in range(4)])


def dp_hop(values, step):
    size = lax.axis_size("dp")
    return lax.ppermute(values, "dp", [(i, i ^ step) for i in range(size)])


def time_features(moments, width):
    half = width // 2
    rates = jnp.exp(-math.log(10000.0) * jnp.arange(half, dtype=F32) / half)
    angles = moments.astype(F32)[:, None] * rates[None, :]
    return jnp.concatenate([jnp.cos(angles), jnp.sin(angles)], axis=1)


def shards(
    tokens,
    text,
    timesteps,
    item_frames,
    cotangent,
    self_query,
    self_query_bias,
    self_key,
    self_value,
    self_value_bias,
    self_output,
    self_output_bias,
    cross_query,
    cross_query_bias,
    cross_key,
    cross_value,
    cross_value_bias,
    cross_output,
    cross_output_bias,
    hidden_up,
    hidden_up_bias,
    hidden_down,
    hidden_down_bias,
    modulation,
    modulation_bias,
):
    frames, width = tokens.shape
    words = text.shape[1]
    columns = modulation.shape[2]
    narrow = self_query.shape[2]
    units = hidden_up.shape[2]
    rank = lax.axis_index("tensor")
    me = lax.axis_index("dp")
    size = lax.axis_size("dp")
    core = rank % 2
    share = frames // 2
    blocks = share // UNIT
    unit = width // size
    turn = lambda values: jnp.swapaxes(values, 1, 2)

    order = jnp.arange(SLOTS, dtype=jnp.int32)
    ends = jnp.sum(jnp.where(order[:, None] <= order[None, :], item_frames[:, None], 0), axis=0)
    turned = (jnp.arange(frames // UNIT, dtype=jnp.int32) + core * blocks) % (2 * blocks)
    slots = jnp.sum((turned[:, None] * UNIT >= ends[None, :]).astype(jnp.int32), axis=1)
    places = jnp.stack([rank, rank // 2, rank ^ 1, me]).astype(jnp.int32)
    info = jnp.concatenate([(rank * 2 + me % 2)[None].astype(jnp.int32), slots, places])

    def pack(members, whole, after=()):
        rows = [sum(a.shape[1] for a in some) for _, some in members]
        outs = [shape(r, width, dtype=BF) for r, one in zip(rows, whole) if one]
        outs += [shape(r // 2, width, dtype=BF) for r in rows]
        arrays = [a for _, some in members for a in some]
        results = pl.pallas_call(
            partial(
                pack_kernel,
                groups=[(layer, [None] * len(some)) for layer, some in members],
                whole=whole,
                after=len(after),
            ),
            out_shape=outs,
            in_specs=[SMALL] + [ANY] * (len(arrays) + len(after)),
            out_specs=[ANY] * len(outs),
            scratch_shapes=[
                *[pltpu.VMEM((r, width), BF) for r in rows],
                pltpu.SemaphoreType.DMA((4 * len(members),)),
                pltpu.SemaphoreType.DMA((2 * len(members),)),
            ],
            compiler_params=pltpu.CompilerParams(vmem_limit_bytes=VMEM_BYTES),
            cost_estimate=lasting(1.0),
            name="pack_weights",
        )(info, *arrays, *after)
        return list(results[: sum(whole)]), list(results[sum(whole) :])

    selfs = [turn(self_query), turn(self_key), turn(self_value), self_output]
    crosses = [turn(cross_query), turn(cross_key), turn(cross_value), cross_output]
    own0, first0 = pack([(0, selfs)], [True])


    condition = jax.nn.silu(time_features(timesteps, width)).astype(BF)
    mine = plain(
        mod_kernel,
        "mod_rows",
        None,
        [
            condition,
            turn(modulation),
            modulation_bias,
            self_query_bias,
            self_value_bias,
            cross_query_bias,
            cross_value_bias,
            hidden_up_bias,
        ],
        [shape(LAYERS, 8, -(-columns // LANES) * LANES)],
    )
    own1, first1 = pack(
        [(0, crosses), (1, selfs), (1, crosses), (1, [hidden_up]), (1, [hidden_down])],
        [True, True, True, False, False],
        [mine],
    )
    firsts, owns = first0 + first1, own0 + own1
    others = [tensor_hop(mine, 1), tensor_hop(mine, 2)]
    others.append(tensor_hop(others[0], 2))
    out_biases = [
        b.reshape(LAYERS, 1, width) for b in (self_output_bias, cross_output_bias, hidden_down_bias)
    ]

    count = len(firsts)
    along_x, along_y, over_x, over_y, sibs = [[None] * count for _ in range(5)]

    def leave(index):
        along_x[index] = tensor_hop(firsts[index], 2)

    def swap(index):
        sibs[index] = tensor_hop(owns[index], 1)

    def go_on(index):
        along_y[index] = dp_hop(along_x[index], 1)
        over_x[index] = tensor_hop(along_x[index], 1)

    def end(index):
        over_y[index] = tensor_hop(along_y[index], 1)

    def weights_of(index):
        return [
            owns[index],
            sibs[index],
            along_x[index],
            along_y[index],
            over_x[index],
            over_y[index],
        ]

    def open_gate(after, leaving=(), at_x=(), at_y=(), settled=()):
        places = [(firsts, i) for i in leaving]
        places += [(along_x, i) for i in at_x] + [(along_y, i) for i in at_y] + list(settled)
        opened = gate([values[i] for values, i in places], after)
        for (values, i), array in zip(places, opened):
            values[i] = array
        for i in leaving:
            leave(i)
        for i in at_x:
            go_on(i)
        for i in at_y:
            end(i)
        return list(opened)

    leave(0)
    swap(0)
    open_gate([mine], [], [0])
    open_gate([*others, along_x[0]], [1])
    swap(1)
    go_on(1)
    owns += [hidden_up, hidden_down]
    sibs[4:6] = tensor_hop(hidden_up, 1), tensor_hop(hidden_down, 1)
    mods, narrow_biases, up_biases = plain(
        partial(assemble_kernel, narrow=narrow, units=units, columns=columns),
        "mod_all",
        info,
        [mine, *others],
        [
            shape(LAYERS, SLOTS, 4 * columns),
            shape(LAYERS, 8, 4 * narrow),
            shape(LAYERS, 1, 4 * units),
        ],
        after=[along_x[1]],
    )
    open_gate([mods], [], [], [0])

    text_rows = jnp.pad(text, ((0, 0), (0, LANES - words), (0, 0))).reshape(-1, width)
    whole = pltpu.VMEM((width, width), BF)
    four = pltpu.VMEM((4, width, units), BF)
    two = pltpu.VMEM((2, width, units), BF)
    floats = pltpu.VMEM((share, width), F32)
    lows = pltpu.VMEM((share, width), BF)
    sems = lambda n: pltpu.SemaphoreType.DMA((n,))
    frame_low = shape(share, width, dtype=BF)
    frame_high = shape(share, width)
    frame_wide = shape(share, 4 * units, dtype=BF)
    frame_chip = shape(share, 2 * units, dtype=BF)
    two_low = shape(2, share, width, dtype=BF)
    two_text = shape(2, SLOTS * LANES, width, dtype=BF)
    logs = shape(16, share)
    log_work = pltpu.VMEM((share, LANES), F32)
    stat_shape = shape(72, width)

    kept = []
    for layer in range(LAYERS):
        first = 2 * layer
        mod = (mods, (layer,))
        biases = (narrow_biases, (layer,))
        common = dict(w=pltpu.VMEM((2, width, width), BF), sems=sems(8))
        if layer == 0:
            entry1, kv, x = run(
                kv_kernel,
                "self_kv",
                info,
                {},
                dict(mod=mod, biases=biases),
                weights_of(first) + [tokens],
                dict(entry=frame_low, kv=two_low, x=frame_high),
                {},
                common | dict(rows=lows, row_sems=sems(1)),
                [along_x[1], sibs[1], sibs[4], sibs[5]],
                3.0,
            )
        else:
            entry1, kv, x, branch3 = run(
                kv_kernel,
                "residual_kv",
                info,
                dict(part=part, other=tensor_hop(part, 2), below=kept[-1]["x2"]),
                dict(
                    mod=mod,
                    mod_below=(mods, (layer - 1,)),
                    bias=(out_biases[2], (layer - 1,)),
                    biases=biases,
                ),
                weights_of(first),
                dict(entry=frame_low, kv=two_low, x=frame_high, branch=frame_low),
                {},
                common | dict(sum=floats),
                opened,
                3.0,
            )
            kept[-1]["branch3"] = branch3
        kv_sib = tensor_hop(kv, 1)
        opened = (
            open_gate([entry1], [2, 3], [], [], [(over_x, 1)])
            if layer == 0
            else open_gate([entry1], [5], [], [], [(over_x, 4), (over_y, 3)])
        )
        (q,) = run(
            q_kernel,
            "query",
            info,
            dict(entry=entry1),
            dict(biases=biases),
            weights_of(first),
            dict(q=frame_low),
            {},
            dict(w=whole, sems=sems(4)),
            [],
            15.0,
        )
        x1, mixed1, rest1, lse1, branch1 = run(
            self_kernel,
            "self",
            info,
            dict(q=q, kv_own=kv, kv_sib=kv_sib, x=x),
            dict(mod=mod, bias=(out_biases[0], (layer,))),
            weights_of(first),
            dict(out=frame_high, mixed=frame_low, rest=frame_low, lse=logs, branch=frame_low),
            {},
            dict(wo=whole, logs=log_work, sum=floats, sems=sems(4)),
            opened,
            8.0,
        )
        if layer == 0:
            opened = open_gate([x1], [4], [2], [1], [(along_x, 3)])
            swap(2)
        else:
            opened = open_gate([x1], [], [5], [4])
        x2, entry2, cq, ckv, mixed2, lse2, branch2 = run(
            partial(cross_kernel, words=words),
            "cross",
            info,
            dict(x=x1, text=text_rows),
            dict(mod=mod, biases=biases, bias=(out_biases[1], (layer,))),
            weights_of(first + 1),
            dict(
                out=frame_high,
                entry=frame_low,
                q=frame_low,
                kv=two_text,
                mixed=frame_low,
                lse=logs,
                branch=frame_low,
            ),
            {},
            dict(
                wq=whole, wk=whole, wv=whole, wo=whole, logs=log_work, sum=floats, sems=sems(16)
            ),
            opened,
            6.0,
        )
        if layer == 0:
            opened = open_gate([x2], [], [3], [2], [(over_x, 2), (sibs, 2), (along_x, 4)])
            swap(3)
        else:
            opened = open_gate([x2], [], [], [5], [(over_x, 5), (over_y, 4)])
        if layer == 0:
            part, entry3, active, slope = run(
                lambda info, work, w: hidden_kernel(info, work, w, 0),
                "ff_part",
                info,
                dict(x=x2),
                dict(mod=mod, up_bias=(up_biases, (layer,))),
                [hidden_up, sibs[4], hidden_down, sibs[5]],
                dict(part=frame_low, entry=frame_low, active=frame_chip, slope=frame_chip),
                {},
                dict(
                    up=two, down=two, before=floats, sum=floats, sems=sems(2), down_sems=sems(2)
                ),
                opened,
                5.0,
            )
            opened = open_gate([part], [], [4], [3], [(over_x, 3), (over_y, 2), (sibs, 3)])
            x3 = branch3 = None
        else:
            x3 = branch3 = active = slope = entry3 = None
        kept.append(
            dict(
                x=x,
                entry1=entry1,
                q=q,
                kv=kv,
                kv_sib=kv_sib,
                mixed1=mixed1,
                rest1=rest1,
                lse1=lse1,
                branch1=branch1,
                x1=x1,
                entry2=entry2,
                cq=cq,
                ckv=ckv,
                mixed2=mixed2,
                lse2=lse2,
                branch2=branch2,
                x2=x2,
                entry3=entry3,
                active=active,
                slope=slope,
                branch3=branch3,
            )
        )
        x = x3
    last_gate = opened

    def join(rows, *after):
        return plain(
            join_kernel,
            "join_rows",
            info,
            [rows, tensor_hop(rows, 1)],
            [shape(2 * share, width, dtype=BF)],
            after=after,
        )


    chains = {}

    def start(name, send, keep):
        view = (size, unit, send.shape[1])
        chains[name] = (tensor_hop(send, 1).reshape(view), keep.reshape(view), 0)

    def held(*names):
        return [chains[name][1] for name in names]

    def advance(names, after=(), cost=1.5):
        targets = [(n, [n]) if isinstance(n, str) else n for n in names]
        targets = [t for t in targets if 2 ** chains[t[1][0]][2] < size]
        if not targets:
            return
        ins, in_specs, outs, out_specs, spots = [], [], [], [], []
        for result, (_, parts) in enumerate(targets):
            column = 0
            for name in parts:
                received, kept_part, bit = chains[name]
                blocks_left, rows, wide = received.shape
                spots.append((result, column))
                column += wide
                for side in range(2):

                    def at(i, info, bit=bit, side=side):
                        return (0, ((info[8] >> bit) & 1) ^ side, 0, 0)

                    for part in (received, kept_part):
                        ins.append(part.reshape(blocks_left // 2, 2, rows, wide))
                        in_specs.append(pl.BlockSpec((blocks_left // 2, None, rows, wide), at))
            for side in range(2):
                outs.append(shape(blocks_left // 2, rows, column, dtype=BF))
                out_specs.append(
                    pl.BlockSpec((blocks_left // 2, rows, column), lambda i, info: (0, 0, 0))
                )
        results = pl.pallas_call(
            partial(merge_kernel, spots=spots, after=len(after)),
            grid_spec=pltpu.PrefetchScalarGridSpec(
                num_scalar_prefetch=1,
                grid=(1,),
                in_specs=in_specs + [ANY] * len(after),
                out_specs=out_specs,
            ),
            out_shape=outs,
            compiler_params=pltpu.CompilerParams(vmem_limit_bytes=VMEM_BYTES),
            cost_estimate=lasting(cost),
            name="merge_grads",
        )(info, *ins, *after)
        for index, (name, parts) in enumerate(targets):
            bit = chains[parts[0]][2]
            hold, give = results[2 * index : 2 * index + 2]
            for part in parts:
                del chains[part]
            chains[name] = (dp_hop(give, 2**bit), hold, bit + 1)

    sums = []
    last = LAYERS - 1
    for layer in reversed(range(LAYERS)):
        first = 2 * layer
        k = kept[layer]
        mod = (mods, (layer,))
        above = layer + 1
        f_name, c_name, a_name, s_name = [f"{kind}{layer}" for kind in "fcas"]
        n_name = f"n{above}"

        def grads_out(members):
            return dict.fromkeys(SIDES, shape(width, members * narrow, dtype=BF))

        older = []
        if layer < last:
            older = [f"f{above}", n_name]
            more = held(*older)
        if layer == last:
            f_send, f_keep, low, c_send, c_keep, g, stats = run(
                lambda info, work, w: hidden_cross_kernel(info, work, w, words),
                "ff_cross_back",
                info,
                dict(
                    x2=k["x2"],
                    branch2=k["branch2"],
                    q=k["cq"],
                    kv=k["ckv"],
                    lse=k["lse2"],
                    entry2=k["entry2"],
                    text=text_rows,
                    mixed=k["mixed2"],
                    x1=k["x1"],
                ),
                dict(mod=mod, up_bias=(up_biases, (layer,)), bias=(out_biases[2], (layer,))),
                weights_of(4) + weights_of(5) + [cotangent] + weights_of(first + 1),
                {f"f_{name}": shape(width, 2 * units, dtype=BF) for name in SIDES}
                | dict(low=frame_low)
                | {f"c_{name}": shape(width, 4 * narrow, dtype=BF) for name in SIDES}
                | dict(out=frame_high),
                dict(stats=stat_shape),
                dict(
                    up=four,
                    down=four,
                    g=floats,
                    g_mid=floats,
                    rows=lows,
                    row_sems=sems(1),
                    gb=lows,
                    entry3=lows,
                    branch3=lows,
                    active=pltpu.VMEM((share, 4 * units), BF),
                    slope=pltpu.VMEM((share, 4 * units), BF),
                    d_before=pltpu.VMEM((share, 4 * units), BF),
                    before=floats,
                    sum=floats,
                    sems=sems(8),
                    down_sems=sems(8),
                    wq=whole,
                    wo=whole,
                    dkv=pltpu.VMEM(two_text.shape, BF),
                    dkv_sum=pltpu.VMEM(two_text.shape, F32),
                    csems=sems(8),
                ),
                last_gate,
                10.0,
            )
            start(f_name, f_send, f_keep)
            start(c_name, c_send, c_keep)
        else:
            part, gb, d_before, stats = run(
                lambda info, work, w: hidden_back_kernel(info, work, w, 0),
                "ff_back",
                info,
                dict(g=g, branch=k["branch3"], slope=k["slope"]),
                dict(mod=mod),
                [hidden_up, sibs[4], hidden_down, sibs[5]],
                dict(part=frame_low, gb=frame_low, d_before=frame_chip),
                dict(stats=stat_shape),
                dict(
                    up=two, down=two, before=floats, de=floats, sems=sems(2), down_sems=sems(2)
                ),
                more,
                5.0,
            )
            other = tensor_hop(part, 2)
            send, keep = run(
                hidden_grads_kernel,
                "ff_grads",
                info,
                dict(entry=k["entry3"], d_before=d_before, gb=gb, active=k["active"]),
                {},
                [],
                dict.fromkeys(SIDES, shape(width, 2 * units, dtype=BF)),
                {},
                {},
                [gb],
                1.0,
            )
            start(f_name, send, keep)
            output = join(low, gb)
            advance(older, held(f_name), 0.5)
            extra = dict(part=part, other=other, above=k["x2"])
            scratch = dict(g_mid=floats)
        if layer < last:
            send, keep, g, stats = run(
                partial(cross_back_kernel, words=words),
                "cross_back",
                info,
                dict(
                    g=g,
                    branch=k["branch2"],
                    q=k["cq"],
                    kv=k["ckv"],
                    lse=k["lse2"],
                    entry=k["entry2"],
                    text=text_rows,
                    mixed=k["mixed2"],
                    x=k["x1"],
                    **extra,
                ),
                dict(mod=mod, early=(stats, ())),
                weights_of(first + 1),
                grads_out(4) | dict(out=frame_high),
                dict(stats=stat_shape),
                dict(
                    wq=whole,
                    wo=whole,
                    gb=lows,
                    dq=lows,
                    dkv=pltpu.VMEM(two_text.shape, BF),
                    d_mixed=lows,
                    de=floats,
                    dkv_sum=pltpu.VMEM(two_text.shape, F32),
                    sems=sems(8),
                    **scratch,
                ),
                held(f_name, *older) + [output],
                60.0,
            )
            start(c_name, send, keep)
            advance([f_name, n_name], [g, chains[f"f{above}"][0]])
        gb1, dq, dkv_own, dkv_give, stats = run(
            self_back_kernel,
            "self_back",
            info,
            dict(
                g=g,
                branch=k["branch1"],
                mixed=k["mixed1"],
                rest=k["rest1"],
                q=k["q"],
                kv_own=k["kv"],
                kv_sib=k["kv_sib"],
                lse=k["lse1"],
            ),
            dict(mod=mod, early=(stats, ())),
            weights_of(first),
            dict(gb=frame_low, dq=frame_low, dkv_own=two_low, dkv_give=two_low),
            dict(stats=stat_shape),
            dict(wo=whole, d_mixed=lows, inner=pltpu.VMEM((16, share), F32), sems=sems(4)),
            held(f_name, c_name, *([n_name] if layer < last else [])),
            13.0,
        )
        dkv_sib = tensor_hop(dkv_give, 1)
        if layer == last:
            advance([f_name], [dq])
        else:
            advance([f_name, c_name], [dq, chains[n_name][0]])
        send, keep = run(
            query_output_kernel,
            "qo_grads",
            info,
            dict(entry=k["entry1"], gb=gb1, dq=dq, mixed=k["mixed1"]),
            {},
            [],
            grads_out(2),
            {},
            {},
            held(f_name, c_name),
            60.0,
        )
        start(a_name, send, keep)
        arriving = dict(dkv_own=dkv_own, dkv_sib=dkv_sib, entry=k["entry1"])
        if layer == 0:
            send, keep, dkv = run(
                kv_grads_kernel,
                "kv_grads",
                info,
                arriving,
                {},
                [],
                grads_out(2) | dict(dkv=two_low),
                {},
                {},
                held(a_name),
                4.0,
            )
            start(s_name, send, keep)
            rest = f"t{layer}"
            advance([f_name, c_name, (rest, [a_name, s_name])], held(s_name))
            arriving = dict(dkv=dkv)
        results = run(
            qkv_back_kernel,
            "qkv_back",
            info,
            arriving | dict(dq=dq, x=k["x"], g=g),
            dict(mod=mod, early=(stats, ())),
            weights_of(first),
            (dict(low=frame_low) if layer == 0 else grads_out(2)) | dict(out=frame_high),
            dict(stats=stat_shape),
            dict(wq=whole, wk=whole, wv=whole, de=floats, sems=sems(12))
            | (dict(dkv=pltpu.VMEM(two_low.shape, BF)) if layer else {}),
            held(f_name, c_name, rest if layer == 0 else a_name),
            6.0,
        )
        g, stats = results[-2:]
        if layer:
            start(s_name, *results[:2])
        if layer:
            advance([f_name, (f"n{layer}", [c_name, a_name, s_name])], [g])
        else:
            to_rest = [g, chains[f_name][0]]
        sums = [stats, tensor_hop(stats, 1)] + sums
    vectors = plain(
        partial(collect_kernel, narrow=narrow, units=units, columns=columns),
        "collect",
        info,
        [*sums, condition],
        [shape(16, mine.shape[2], dtype=BF)],
        [pltpu.VMEM(stat_shape.shape, F32), pltpu.VMEM((16, mine.shape[2]), F32)],
    )
    advance(["c0", "t0"], to_rest + [vectors])
    gathered, hop = vectors[None], size // 2

    def gather_sums():
        nonlocal gathered, hop
        if hop:
            both = jnp.stack([gathered, dp_hop(gathered, hop)], axis=1)
            gathered = both.reshape(-1, *vectors.shape)
            hop //= 2

    low = results[0]
    (low,) = gate([low], held("t0"))
    input_grad = join(low)

    def parts_of(*names):
        return [part.reshape(1, unit, -1) for name in names for part in chains[name][:2]]

    up_grad, down_grad = plain(
        partial(finish_kernel, wide=True, spots=[(0, [(0, 0)]), (0, [(1, 0)])]),
        "wide",
        None,
        parts_of("f0", "f1"),
        [shape(LAYERS, unit, units)] * 2,
    )
    ready = [input_grad, up_grad, chains["c0"][0]]
    while any(2 ** chain[2] < size for chain in chains.values()):
        gather_sums()
        advance(list(chains), held("t0") + [gathered] + ready)
    while hop:
        gather_sums()
    straight, across = shape(LAYERS, unit, narrow), shape(LAYERS, narrow, unit)
    spots = [(0, [(1, 0), (1, 1), (1, 2), (1, 3)])]
    spots += [(0, [(0, 0), (0, 1)]), (0, [(0, 2), (0, 3)])]
    cq_grad, ck_grad, cv_grad, co_grad, q_grad, o_grad, k_grad, v_grad = plain(
        partial(finish_kernel, wide=False, spots=spots),
        "narrow",
        None,
        parts_of("n1", "c0", "t0"),
        [straight, straight, straight, across, straight, across, straight, straight],
    )
    small = plain(
        spread_kernel,
        "spread",
        info,
        [gathered],
        [shape(LAYERS, unit, columns), shape(LAYERS, columns)]
        + [shape(LAYERS, narrow)] * 4
        + [shape(LAYERS, units)]
        + [shape(LAYERS, unit)] * 3,
        [pltpu.VMEM((SLOTS * size, columns), F32), pltpu.VMEM((SLOTS * size, width), F32)],
    )
    mod_grad, mod_bias_grad, q_sum, v_sum, cq_sum, cv_sum, up_sum, o1, o2, o3 = small
    return (
        output,
        input_grad,
        q_grad,
        q_sum,
        k_grad,
        v_grad,
        v_sum,
        o_grad,
        o1,
        cq_grad,
        cq_sum,
        ck_grad,
        cv_grad,
        cv_sum,
        co_grad,
        o2,
        up_grad,
        up_sum,
        turn(down_grad),
        o3,
        mod_grad,
        mod_bias_grad,
    )


def solution(mesh):
    dp, tensor = "dp", "tensor"
    columns, vector = P(None, None, tensor), P(None, tensor)
    matrix, turned, spread = P(None, dp, tensor), P(None, tensor, dp), P(None, dp)
    placed = (
        P(dp, None),
        P(dp, None, None),
        P(dp),
        P(dp),
        P(dp, None),
        columns,
        vector,
        columns,
        columns,
        vector,
        P(None, tensor, None),
        P(),
        columns,
        vector,
        columns,
        columns,
        vector,
        P(None, tensor, None),
        P(),
        columns,
        vector,
        P(None, tensor, None),
        P(),
        columns,
        vector,
    )
    results = (
        P(dp, None),
        P(dp, None),
        matrix,
        vector,
        matrix,
        matrix,
        vector,
        turned,
        spread,
        matrix,
        vector,
        matrix,
        matrix,
        vector,
        turned,
        spread,
        matrix,
        vector,
        turned,
        spread,
        matrix,
        vector,
    )
    return jax.shard_map(
        shards, mesh=mesh, in_specs=placed, out_specs=results, check_vma=False
    )
```

profile of v0, /device:TPU:0, one launch (start us, length us, event | category | flops | bytes accessed | tf_op | source)
XLA Modules:
  0.0 473.5 jit_solution(7581628624619606494)
XLA Ops:
  16.9 5.7 %pack_weights.2 = (bf16[768,768]{1,0:T(8,128)(2,1)}, bf16[768,768]{1,0:T(8,128)(2,1)}, bf16[768,768]{1,0:T(8,128)(2,1)}, bf16[384,768]{1,0:T(8,128)(2,1)}, bf16[...) custom-call(s32[9]{0:T(128)} %concatenate.6.info.refs_0_, ...), custom_call_target="tpu_custom_call" | custom-call | flops 400000000 | bytes 1000 | tf_op jit(solution)/shard_map/pack_weights/pallas_call | solution.py:1309
  29.3 9.7 %collective-permute-done.6.refs_0_ = bf16[384,768]{1,0:T(8,128)(2,1)S(1)} collective-permute-done((bf16[384,768]{1,0:T(8,128)(2,1)}, bf16[384,768]{1,0:T(8,128)(2,1)S(1)}, u32[]{:S(2)}, u32[]{:S(2)}) %collective-permute-start.6) | collective-permute-done | bytes 589856 | tf_op jit(solution)/shard_map/ppermute | solution.py:1246
  48.3 6.6 %self_kv.1 = (bf16[512,768]{1,0:T(8,128)(2,1)}, bf16[2,512,768]{2,1,0:T(8,128)(2,1)}, f32[512,768]{1,0:T(8,128)}) custom-call(s32[9]{0:T(128)} %concatenate.6.info.refs_0_, f32[2,4,6912]{2,1,0:T(4,128)} %get-tuple-element.188.refs_1_.refs_5_.refs_3_.refs_2_.refs_4_.refs_10_.refs_9_.refs_7_.refs_13_, f32[2,8,768]{2,1,0:T(8,128)} %get-tuple-element.189.refs_2_.refs_4_.refs_7_, ...), custom_call_target="tpu_custom_call" | custom-call | flops 1200000000 | bytes 1000 | tf_op jit(solution)/shard_map/self_kv/pallas_call | solution.py:162
  67.6 17.5 %self.2 = (f32[512,768]{1,0:T(8,128)}, bf16[512,768]{1,0:T(8,128)(2,1)}, bf16[512,768]{1,0:T(8,128)(2,1)}, f32[16,512]{1,0:T(8,128)}, bf16[512,768]{1,0:T(8,128)(2,1)}) custom-call(s32[9]{0:T(128)} %concatenate.6.info.refs_0_, bf16[512,768]{1,0:T(8,128)(2,1)} %query.2.refs_1_.refs_5_, bf16[2,512,768]{2,1,0:T(8,128)(2,1)} %get-tuple-element.193.refs_2_.refs_6_, ...), custom_call_target="tpu_custom_call" | custom-call | flops 3200000000 | bytes 1000 | tf_op jit(solution)/shard_map/self/pallas_call | solution.py:162
  94.5 13.9 %cross.2 = (f32[512,768]{1,0:T(8,128)}, bf16[512,768]{1,0:T(8,128)(2,1)}, bf16[512,768]{1,0:T(8,128)(2,1)}, bf16[2,512,768]{2,1,0:T(8,128)(2,1)}, bf16[512,768]{...) custom-call(s32[9]{0:T(128)} %concatenate.6.info.refs_0_, ...), custom_call_target="tpu_custom_call" | custom-call | flops 2400000000 | bytes 1000 | tf_op jit(solution)/shard_map/cross/pallas_call | solution.py:162
  109.3 9.8 %ff_part.1 = (bf16[512,768]{1,0:T(8,128)(2,1)}, bf16[512,768]{1,0:T(8,128)(2,1)}, bf16[512,1536]{1,0:T(8,128)(2,1)}, bf16[512,1536]{1,0:T(8,128)(2,1)}) custom-call(s32[9]{0:T(128)} %concatenate.6.info.refs_0_, f32[512,768]{1,0:T(8,128)} %get-tuple-element.206.refs_5_.refs_1_.refs_3_.refs_12_, ...), custom_call_target="tpu_custom_call" | custom-call | flops 2000000000 | bytes 1000 | tf_op jit(solution)/shard_map/ff_part/pallas_call | solution.py:162
  121.9 13.7 %collective-permute-done.23.refs_1_ = bf16[384,768]{1,0:T(8,128)(2,1)S(1)} collective-permute-done((bf16[384,768]{1,0:T(8,128)(2,1)}, bf16[384,768]{1,0:T(8,128)(2,1)S(1)}, u32[]{:S(2)}, u32[]{:S(2)}) %collective-permute-start.23) | collective-permute-done | bytes 589856 | tf_op jit(solution)/shard_map/ppermute | solution.py:1246
  139.4 7.8 %residual_kv.1 = (bf16[512,768]{1,0:T(8,128)(2,1)}, bf16[2,512,768]{2,1,0:T(8,128)(2,1)}, f32[512,768]{1,0:T(8,128)}, bf16[512,768]{1,0:T(8,128)(2,1)}) custom-call(s32[9]{0:T(128)} %concatenate.6.info.refs_0_, bf16[512,768]{1,0:T(8,128)(2,1)} %get-tuple-element.214.refs_5_.refs_1_, bf16[512,768]{1,0:T(8,128)(2,1)} %collective-permute-done.22.refs_2_, ...), custom_call_target="tpu_custom_call" | custom-call | flops 1200000000 | bytes 1000 | tf_op jit(solution)/shard_map/residual_kv/pallas_call | solution.py:162
  158.3 17.1 %self.3 = (f32[512,768]{1,0:T(8,128)}, bf16[512,768]{1,0:T(8,128)(2,1)}, bf16[512,768]{1,0:T(8,128)(2,1)}, f32[16,512]{1,0:T(8,128)}, bf16[512,768]{1,0:T(8,128)(2,1)}) custom-call(s32[9]{0:T(128)} %concatenate.6.info.refs_0_, bf16[512,768]{1,0:T(8,128)(2,1)} %query.3.refs_1_.refs_5_, bf16[2,512,768]{2,1,0:T(8,128)(2,1)} %get-tuple-element.222.refs_2_.refs_6_, ...), custom_call_target="tpu_custom_call" | custom-call | flops 3200000000 | bytes 1000 | tf_op jit(solution)/shard_map/self/pallas_call | solution.py:162
  177.3 14.2 %cross.3 = (f32[512,768]{1,0:T(8,128)}, bf16[512,768]{1,0:T(8,128)(2,1)}, bf16[512,768]{1,0:T(8,128)(2,1)}, bf16[2,512,768]{2,1,0:T(8,128)(2,1)}, bf16[512,768]{...) custom-call(s32[9]{0:T(128)} %concatenate.6.info.refs_0_, ...), custom_call_target="tpu_custom_call" | custom-call | flops 2400000000 | bytes 1000 | tf_op jit(solution)/shard_map/cross/pallas_call | solution.py:162
  195.3 37.4 %ff_cross_back.1 = (bf16[768,1536]{1,0:T(8,128)(2,1)}, bf16[768,1536]{1,0:T(8,128)(2,1)}, bf16[512,768]{1,0:T(8,128)(2,1)}, bf16[768,768]{1,0:T(8,128)(2,1)}, bf...) custom-call(s32[9]{0:T(128)} %concatenate.6.info.refs_0_, ...), custom_call_target="tpu_custom_call" | custom-call | flops 4000000000 | bytes 1000 | tf_op jit(solution)/shard_map/ff_cross_back/pallas_call | solution.py:162
  233.5 26.2 %self_back.2 = (bf16[512,768]{1,0:T(8,128)(2,1)}, bf16[512,768]{1,0:T(8,128)(2,1)}, bf16[2,512,768]{2,1,0:T(8,128)(2,1)}, bf16[2,512,768]{2,1,0:T(8,128)(2,1)}, f32[72,768]{1,0:T(8,128)}) custom-call(s32[9]{0:T(128)} %concatenate.6.info.refs_0_, f32[512,768]{1,0:T(8,128)} %get-tuple-element.242.refs_1_.refs_6_, bf16[512,768]{1,0:T(8,128)(2,1)} %get-tuple-element.243.refs_2_, ...), custom_call_target="tpu_custom_call" | custom-call | flops 5200000000 | bytes 1000 | tf_op jit(solution)/shard_map/self_back/pallas_call | solution.py:162
  266.3 5.0 %qo_grads.2 = (bf16[768,384]{1,0:T(8,128)(2,1)}, bf16[768,384]{1,0:T(8,128)(2,1)}) custom-call(s32[9]{0:T(128)} %concatenate.6.info.refs_0_, bf16[512,768]{1,0:T(8,128)(2,1)} %get-tuple-element.221.refs_1_.refs_3_, bf16[512,768]{1,0:T(8,128)(2,1)} %get-tuple-element.256.refs_2_, bf16[512,768]{1,0:T(8,128)(2,1)} %get-tuple-element.252.refs_4_.refs_3_, ...), custom_call_target="tpu_custom_call" | custom-call | flops 24000000000 | bytes 1000 | tf_op jit(solution)/shard_map/qo_grads/pallas_call | solution.py:162
  271.3 12.4 %qkv_back.2 = (bf16[768,384]{1,0:T(8,128)(2,1)}, bf16[768,384]{1,0:T(8,128)(2,1)}, f32[512,768]{1,0:T(8,128)}, f32[72,768]{1,0:T(8,128)}) custom-call(s32[9]{0:T(128)} %concatenate.6.info.refs_0_, bf16[2,512,768]{2,1,0:T(8,128)(2,1)} %get-tuple-element.250.refs_1_, bf16[2,512,768]{2,1,0:T(8,128)(2,1)} %collective-permute-done.37.refs_2_, ...), custom_call_target="tpu_custom_call" | custom-call | flops 2400000000 | bytes 1000 | tf_op jit(solution)/shard_map/qkv_back/pallas_call | solution.py:162
  286.9 6.2 %collective-permute-done.39 = bf16[4,96,1536]{2,1,0:T(8,128)(2,1)} collective-permute-done((bf16[4,96,1536]{2,1,0:T(8,128)(2,1)}, bf16[4,96,1536]{2,1,0:T(8,128)(2,1)}, u32[]{:S(2)}, u32[]{:S(2)}) %collective-permute-start.39) | collective-permute-done | bytes 1179680 | tf_op jit(solution)/shard_map/ppermute | solution.py:1246
  293.1 5.8 %merge_grads.9 = (bf16[2,96,1536]{2,1,0:T(8,128)(2,1)}, bf16[2,96,1536]{2,1,0:T(8,128)(2,1)}, bf16[4,96,1536]{2,1,0:T(8,128)(2,1)}, bf16[4,96,1536]{2,1,0:T(8,128)(2,1)}) custom-call(s32[9]{0:T(128)} %concatenate.6.info.refs_0_, bf16[2,2,96,1536]{3,2,1,0:T(8,128)(2,1)} %bitcast.21.refs_0_.refs_2_, bf16[2,2,96,1536]{3,2,1,0:T(8,128)(2,1)} %bitcast.83, ...), custom_call_target="tpu_custom_call" | custom-call | flops 600000000 | bytes 1000 | tf_op jit(solution)/shard_map/merge_grads/pallas_call | solution.py:1642
  300.6 10.8 %ff_back.1 = (bf16[512,768]{1,0:T(8,128)(2,1)}, bf16[512,768]{1,0:T(8,128)(2,1)}, bf16[512,1536]{1,0:T(8,128)(2,1)}, f32[72,768]{1,0:T(8,128)}) custom-call(s32[9]{0:T(128)} %concatenate.6.info.refs_0_, f32[512,768]{1,0:T(8,128)} %get-tuple-element.258.refs_16_.refs_1_, bf16[512,768]{1,0:T(8,128)(2,1)} %get-tuple-element.259.refs_2_, ...), custom_call_target="tpu_custom_call" | custom-call | flops 2000000000 | bytes 1000 | tf_op jit(solution)/shard_map/ff_back/pallas_call | solution.py:162
  316.1 7.4 %ff_grads.1 = (bf16[768,1536]{1,0:T(8,128)(2,1)}, bf16[768,1536]{1,0:T(8,128)(2,1)}) custom-call(s32[9]{0:T(128)} %concatenate.6.info.refs_0_, bf16[512,768]{1,0:T(8,128)(2,1)} %get-tuple-element.277.refs_1_, bf16[512,1536]{1,0:T(8,128)(2,1)} %get-tuple-element.278.refs_2_, bf16[512,768]{1,0:T(8,128)(2,1)} %get-tuple-element.268.refs_3_.refs_5_, ...), custom_call_target="tpu_custom_call" | custom-call | flops 400000000 | bytes 1000 | tf_op jit(solution)/shard_map/ff_grads/pallas_call | solution.py:162
  339.1 19.3 %cross_back.1 = (bf16[768,768]{1,0:T(8,128)(2,1)}, bf16[768,768]{1,0:T(8,128)(2,1)}, f32[512,768]{1,0:T(8,128)}, f32[72,768]{1,0:T(8,128)}) custom-call(s32[9]{0:T(128)} %concatenate.6.info.refs_0_, f32[512,768]{1,0:T(8,128)} %get-tuple-element.258.refs_16_.refs_1_, bf16[512,768]{1,0:T(8,128)(2,1)} %get-tuple-element.269.refs_2_, ...), custom_call_target="tpu_custom_call" | custom-call | flops 24000000000 | bytes 1000 | tf_op jit(solution)/shard_map/cross_back/pallas_call | solution.py:162
  359.4 5.2 %merge_grads.11 = (bf16[4,96,1536]{2,1,0:T(8,128)(2,1)}, bf16[4,96,1536]{2,1,0:T(8,128)(2,1)}, bf16[1,96,1536]{2,1,0:T(8,128)(2,1)}, bf16[1,96,1536]{2,1,0:T(8,128)(2,1)}) custom-call(s32[9]{0:T(128)} %concatenate.6.info.refs_0_, bf16[4,2,96,1536]{3,2,1,0:T(8,128)(2,1)} %bitcast.34.refs_0_.refs_2_, bf16[4,2,96,1536]{3,2,1,0:T(8,128)(2,1)} %bitcast.74, ...), custom_call_target="tpu_custom_call" | custom-call | flops 600000000 | bytes 1000 | tf_op jit(solution)/shard_map/merge_grads/pallas_call | solution.py:1642
  365.2 26.2 %self_back.3 = (bf16[512,768]{1,0:T(8,128)(2,1)}, bf16[512,768]{1,0:T(8,128)(2,1)}, bf16[2,512,768]{2,1,0:T(8,128)(2,1)}, bf16[2,512,768]{2,1,0:T(8,128)(2,1)}, f32[72,768]{1,0:T(8,128)}) custom-call(s32[9]{0:T(128)} %concatenate.6.info.refs_0_, f32[512,768]{1,0:T(8,128)} %get-tuple-element.285.refs_8_.refs_1_.refs_4_, ...), custom_call_target="tpu_custom_call" | custom-call | flops 5200000000 | bytes 1000 | tf_op jit(solution)/shard_map/self_back/pallas_call | solution.py:162
  399.9 5.0 %qo_grads.3 = (bf16[768,384]{1,0:T(8,128)(2,1)}, bf16[768,384]{1,0:T(8,128)(2,1)}) custom-call(s32[9]{0:T(128)} %concatenate.6.info.refs_0_, bf16[512,768]{1,0:T(8,128)(2,1)} %get-tuple-element.192.refs_1_.refs_3_, bf16[512,768]{1,0:T(8,128)(2,1)} %get-tuple-element.299.refs_2_, bf16[512,768]{1,0:T(8,128)(2,1)} %get-tuple-element.300.refs_8_.refs_3_.refs_2_, ...), custom_call_target="tpu_custom_call" | custom-call | flops 24000000000 | bytes 1000 | tf_op jit(solution)/shard_map/qo_grads/pallas_call | solution.py:162
  405.0 5.8 %kv_grads.1 = (bf16[768,384]{1,0:T(8,128)(2,1)}, bf16[768,384]{1,0:T(8,128)(2,1)}, bf16[2,512,768]{2,1,0:T(8,128)(2,1)}) custom-call(s32[9]{0:T(128)} %concatenate.6.info.refs_0_, bf16[2,512,768]{2,1,0:T(8,128)(2,1)} %get-tuple-element.297.refs_1_, bf16[2,512,768]{2,1,0:T(8,128)(2,1)} %collective-permute-done.49.refs_2_, ...), custom_call_target="tpu_custom_call" | custom-call | flops 1600000000 | bytes 1000 | tf_op jit(solution)/shard_map/kv_grads/pallas_call | solution.py:162
  423.3 9.6 %qkv_back.3 = (bf16[512,768]{1,0:T(8,128)(2,1)}, f32[512,768]{1,0:T(8,128)}, f32[72,768]{1,0:T(8,128)}) custom-call(s32[9]{0:T(128)} %concatenate.6.info.refs_0_, bf16[2,512,768]{2,1,0:T(8,128)(2,1)} %get-tuple-element.307.refs_1_, bf16[512,768]{1,0:T(8,128)(2,1)} %get-tuple-element.300.refs_8_.refs_3_.refs_2_, ...), custom_call_target="tpu_custom_call" | custom-call | flops 2400000000 | bytes 1000 | tf_op jit(solution)/shard_map/qkv_back/pallas_call | solution.py:162
  (255 shorter events, 173.9 us)
Async XLA Ops:
  8.5 39.0 %collective-permute-start.10 = (bf16[2,768,768]{2,1,0:T(8,128)(2,1)}, bf16[2,768,768]{2,1,0:T(8,128)(2,1)}, u32[]{:S(2)}, u32[]{:S(2)}) collective-permute-start(bf16[2,768,768]{2,1,0:T(8,128)(2,1)} %refs_5_.3), channel_id=1, source_target_pairs={{0,1},{1,0},{2,3},{3,2},{4,5},{5,4},{6,7},{7,6},{8,9},{9,8},{10,11... | collective-permute-start | bytes 7077896 | tf_op jit(solution)/shard_map/ppermute | solution.py:1241
  8.5 39.0 %collective-permute-start.11 = (bf16[2,768,768]{2,1,0:T(8,128)(2,1)}, bf16[2,768,768]{2,1,0:T(8,128)(2,1)}, u32[]{:S(2)}, u32[]{:S(2)}) collective-permute-start(bf16[2,768,768]{2,1,0:T(8,128)(2,1)} %refs_7_.5), channel_id=1, source_target_pairs={{0,1},{1,0},{2,3},{3,2},{4,5},{5,4},{6,7},{7,6},{8,9},{9,8},{10,11... | collective-permute-start | bytes 7077896 | tf_op jit(solution)/shard_map/ppermute | solution.py:1241
  55.5 52.9 %collective-permute-start.20 = (bf16[768,768]{1,0:T(8,128)(2,1)}, bf16[768,768]{1,0:T(8,128)(2,1)}, u32[]{:S(2)}, u32[]{:S(2)}) collective-permute-start(bf16[768,768]{1,0:T(8,128)(2,1)} %get-tuple-element.208.refs_8_.refs_3_.refs_7_.refs_11_.refs_9_), channel_id=1, source_target_pairs={{0,1},{1,0},{2,3},{3,2},{4,5},{5,4},{6,7},{7,6},{8,9},{9,8},{10,11... | collective-permute-start | bytes 3538952 | tf_op jit(solution)/shard_map/ppermute | solution.py:1241
  56.5 28.6 %collective-permute-start.15 = (bf16[384,768]{1,0:T(8,128)(2,1)}, bf16[384,768]{1,0:T(8,128)(2,1)}, u32[]{:S(2)}, u32[]{:S(2)}) collective-permute-start(bf16[384,768]{1,0:T(8,128)(2,1)} %copy-done.8), channel_id=1, source_target_pairs={{0,4},{4,0},{8,12},{12,8},{16,20},{20,16},{24,28},{28,24},{1,5},{5... | collective-permute-start | bytes 1769480 | tf_op jit(solution)/shard_map/ppermute | solution.py:1246
  61.2 23.9 %collective-permute-start.14 = (bf16[384,768]{1,0:T(8,128)(2,1)}, bf16[384,768]{1,0:T(8,128)(2,1)S(1)}, u32[]{:S(2)}, u32[]{:S(2)}) collective-permute-start(bf16[384,768]{1,0:T(8,128)(2,1)} %get-tuple-element.197.refs_13_), channel_id=1, source_target_pairs={{0,2},{1,3},{2,0},{3,1},{4,6},{5,7},{6,4},{7,5},{8,10},{9,11},{10,... | collective-permute-start | bytes 1769480 | tf_op jit(solution)/shard_map/ppermute | solution.py:1241
  62.6 26.9 %collective-permute-start.16 = (bf16[384,768]{1,0:T(8,128)(2,1)}, bf16[384,768]{1,0:T(8,128)(2,1)}, u32[]{:S(2)}, u32[]{:S(2)}) collective-permute-start(bf16[384,768]{1,0:T(8,128)(2,1)} %get-tuple-element.198.refs_14_), channel_id=1, source_target_pairs={{0,2},{1,3},{2,0},{3,1},{4,6},{5,7},{6,4},{7,5},{8,10},{9,11},{10,... | collective-permute-start | bytes 1769480 | tf_op jit(solution)/shard_map/ppermute | solution.py:1241
  89.6 18.8 %collective-permute-start.21 = (bf16[384,768]{1,0:T(8,128)(2,1)}, bf16[384,768]{1,0:T(8,128)(2,1)}, u32[]{:S(2)}, u32[]{:S(2)}) collective-permute-start(bf16[384,768]{1,0:T(8,128)(2,1)} %get-tuple-element.203.refs_12_), channel_id=1, source_target_pairs={{0,2},{1,3},{2,0},{3,1},{4,6},{5,7},{6,4},{7,5},{8,10},{9,11},{10,... | collective-permute-start | bytes 1769480 | tf_op jit(solution)/shard_map/ppermute | solution.py:1241
  94.4 26.7 %collective-permute-start.26 = (bf16[768,768]{1,0:T(8,128)(2,1)}, bf16[768,768]{1,0:T(8,128)(2,1)}, u32[]{:S(2)}, u32[]{:S(2)}) collective-permute-start(bf16[768,768]{1,0:T(8,128)(2,1)} %get-tuple-element.215.refs_6_.refs_26_), channel_id=1, source_target_pairs={{0,1},{1,0},{2,3},{3,2},{4,5},{5,4},{6,7},{7,6},{8,9},{9,8},{10,11... | collective-permute-start | bytes 3538952 | tf_op jit(solution)/shard_map/ppermute | solution.py:1241
  119.1 20.3 %collective-permute-start.22 = (bf16[512,768]{1,0:T(8,128)(2,1)}, bf16[512,768]{1,0:T(8,128)(2,1)}, u32[]{:S(2)}, u32[]{:S(2)}) collective-permute-start(bf16[512,768]{1,0:T(8,128)(2,1)} %get-tuple-element.214.refs_5_.refs_1_), channel_id=1, source_target_pairs={{0,2},{1,3},{2,0},{3,1},{4,6},{5,7},{6,4},{7,5},{8,10},{9,11},{10,... | collective-permute-start | bytes 2359304 | tf_op jit(solution)/shard_map/ppermute | solution.py:1241
  147.8 27.6 %collective-permute-start.31 = (bf16[384,768]{1,0:T(8,128)(2,1)}, bf16[384,768]{1,0:T(8,128)(2,1)}, u32[]{:S(2)}, u32[]{:S(2)}) collective-permute-start(bf16[384,768]{1,0:T(8,128)(2,1)} %get-tuple-element.217.refs_14_.refs_15_), channel_id=1, source_target_pairs={{0,4},{4,0},{8,12},{12,8},{16,20},{20,16},{24,28},{28,24},{1,5},{5... | collective-permute-start | bytes 1769480 | tf_op jit(solution)/shard_map/ppermute | solution.py:1246
  153.4 22.0 %collective-permute-start.30 = (bf16[384,768]{1,0:T(8,128)(2,1)}, bf16[384,768]{1,0:T(8,128)(2,1)S(1)}, u32[]{:S(2)}, u32[]{:S(2)}) collective-permute-start(bf16[384,768]{1,0:T(8,128)(2,1)} %get-tuple-element.225.refs_13_), channel_id=1, source_target_pairs={{0,2},{1,3},{2,0},{3,1},{4,6},{5,7},{6,4},{7,5},{8,10},{9,11},{10,... | collective-permute-start | bytes 1769480 | tf_op jit(solution)/shard_map/ppermute | solution.py:1241
  232.8 27.3 %collective-permute-start.38 = (bf16[768,1536]{1,0:T(8,128)(2,1)}, bf16[768,1536]{1,0:T(8,128)(2,1)}, u32[]{:S(2)}, u32[]{:S(2)}) collective-permute-start(bf16[768,1536]{1,0:T(8,128)(2,1)} %get-tuple-element.254), channel_id=1, source_target_pairs={{0,1},{1,0},{2,3},{3,2},{4,5},{5,4},{6,7},{7,6},{8,9},{9,8},{10,11... | collective-permute-start | bytes 7077896 | tf_op jit(solution)/shard_map/ppermute | solution.py:1241
  233.4 50.9 %collective-permute-start.40 = (bf16[768,768]{1,0:T(8,128)(2,1)}, bf16[768,768]{1,0:T(8,128)(2,1)}, u32[]{:S(2)}, u32[]{:S(2)}) collective-permute-start(bf16[768,768]{1,0:T(8,128)(2,1)} %get-tuple-element.262), channel_id=1, source_target_pairs={{0,1},{1,0},{2,3},{3,2},{4,5},{5,4},{6,7},{7,6},{8,9},{9,8},{10,11... | collective-permute-start | bytes 3538952 | tf_op jit(solution)/shard_map/ppermute | solution.py:1241
  264.9 28.3 %collective-permute-start.39 = (bf16[4,96,1536]{2,1,0:T(8,128)(2,1)}, bf16[4,96,1536]{2,1,0:T(8,128)(2,1)}, u32[]{:S(2)}, u32[]{:S(2)}) collective-permute-start(bf16[4,96,1536]{2,1,0:T(8,128)(2,1)} %get-tuple-element.261), channel_id=1, source_target_pairs={{0,4},{4,0},{8,12},{12,8},{16,20},{20,16},{24,28},{28,24},{1,5},{5... | collective-permute-start | bytes 3538952 | tf_op jit(solution)/shard_map/ppermute | solution.py:1246
  298.9 31.2 %collective-permute-start.45 = (bf16[4,96,1536]{2,1,0:T(8,128)(2,1)}, bf16[4,96,1536]{2,1,0:T(8,128)(2,1)}, u32[]{:S(2)}, u32[]{:S(2)}) collective-permute-start(bf16[4,96,1536]{2,1,0:T(8,128)(2,1)} %get-tuple-element.282), channel_id=1, source_target_pairs={{0,4},{4,0},{8,12},{12,8},{16,20},{20,16},{24,28},{28,24},{1,5},{5... | collective-permute-start | bytes 3538952 | tf_op jit(solution)/shard_map/ppermute | solution.py:1246
  300.6 22.9 %collective-permute-start.36 = (bf16[512,768]{1,0:T(8,128)(2,1)}, bf16[512,768]{1,0:T(8,128)(2,1)}, u32[]{:S(2)}, u32[]{:S(2)}) collective-permute-start(bf16[512,768]{1,0:T(8,128)(2,1)} %get-tuple-element.241.refs_1_), channel_id=1, source_target_pairs={{0,1},{1,0},{2,3},{3,2},{4,5},{5,4},{6,7},{7,6},{8,9},{9,8},{10,11... | collective-permute-start | bytes 2359304 | tf_op jit(solution)/shard_map/ppermute | solution.py:1241
  311.4 27.6 %collective-permute-start.43 = (bf16[512,768]{1,0:T(8,128)(2,1)}, bf16[512,768]{1,0:T(8,128)(2,1)}, u32[]{:S(2)}, u32[]{:S(2)}) collective-permute-start(bf16[512,768]{1,0:T(8,128)(2,1)} %get-tuple-element.275.refs_10_), channel_id=1, source_target_pairs={{0,2},{1,3},{2,0},{3,1},{4,6},{5,7},{6,4},{7,5},{8,10},{9,11},{10,... | collective-permute-start | bytes 2359304 | tf_op jit(solution)/shard_map/ppermute | solution.py:1241
  323.4 35.1 %collective-permute-start.46 = (bf16[768,1536]{1,0:T(8,128)(2,1)}, bf16[768,1536]{1,0:T(8,128)(2,1)}, u32[]{:S(2)}, u32[]{:S(2)}) collective-permute-start(bf16[768,1536]{1,0:T(8,128)(2,1)} %get-tuple-element.291), channel_id=1, source_target_pairs={{0,1},{1,0},{2,3},{3,2},{4,5},{5,4},{6,7},{7,6},{8,9},{9,8},{10,11... | collective-permute-start | bytes 7077896 | tf_op jit(solution)/shard_map/ppermute | solution.py:1241
  334.9 23.5 %collective-permute-start.48 = (bf16[1,96,1536]{2,1,0:T(8,128)(2,1)}, bf16[1,96,1536]{2,1,0:T(8,128)(2,1)S(1)}, u32[]{:S(2)}, u32[]{:S(2)}) collective-permute-start(bf16[1,96,1536]{2,1,0:T(8,128)(2,1)} %get-tuple-element.293), channel_id=1, source_target_pairs={{0,16},{4,20},{8,24},{12,28},{16,0},{20,4},{24,8},{28,12},{1,17},{... | collective-permute-start | bytes 884744 | tf_op jit(solution)/shard_map/ppermute | solution.py:1246
  337.5 21.0 %collective-permute-start.47 = (bf16[2,96,1536]{2,1,0:T(8,128)(2,1)}, bf16[2,96,1536]{2,1,0:T(8,128)(2,1)S(1)}, u32[]{:S(2)}, u32[]{:S(2)}) collective-permute-start(bf16[2,96,1536]{2,1,0:T(8,128)(2,1)} %get-tuple-element.292), channel_id=1, source_target_pairs={{0,8},{4,12},{8,0},{12,4},{16,24},{20,28},{24,16},{28,20},{1,9},{5... | collective-permute-start | bytes 1769480 | tf_op jit(solution)/shard_map/ppermute | solution.py:1246
  358.4 33.1 %collective-permute-start.51 = (bf16[768,768]{1,0:T(8,128)(2,1)}, bf16[768,768]{1,0:T(8,128)(2,1)}, u32[]{:S(2)}, u32[]{:S(2)}) collective-permute-start(bf16[768,768]{1,0:T(8,128)(2,1)} %get-tuple-element.302), channel_id=1, source_target_pairs={{0,1},{1,0},{2,3},{3,2},{4,5},{5,4},{6,7},{7,6},{8,9},{9,8},{10,11... | collective-permute-start | bytes 3538952 | tf_op jit(solution)/shard_map/ppermute | solution.py:1241
  364.5 28.7 %collective-permute-start.50 = (bf16[4,96,1536]{2,1,0:T(8,128)(2,1)}, bf16[4,96,1536]{2,1,0:T(8,128)(2,1)}, u32[]{:S(2)}, u32[]{:S(2)}) collective-permute-start(bf16[4,96,1536]{2,1,0:T(8,128)(2,1)} %get-tuple-element.301), channel_id=1, source_target_pairs={{0,4},{4,0},{8,12},{12,8},{16,20},{20,16},{24,28},{28,24},{1,5},{5... | collective-permute-start | bytes 3538952 | tf_op jit(solution)/shard_map/ppermute | solution.py:1246
  364.8 26.6 %collective-permute-start.52 = (bf16[1,96,1536]{2,1,0:T(8,128)(2,1)}, bf16[1,96,1536]{2,1,0:T(8,128)(2,1)S(1)}, u32[]{:S(2)}, u32[]{:S(2)}) collective-permute-start(bf16[1,96,1536]{2,1,0:T(8,128)(2,1)} %get-tuple-element.303), channel_id=1, source_target_pairs={{0,16},{4,20},{8,24},{12,28},{16,0},{20,4},{24,8},{28,12},{1,17},{... | collective-permute-start | bytes 884744 | tf_op jit(solution)/shard_map/ppermute | solution.py:1246
  418.5 19.4 %collective-permute-start.58 = (bf16[4,96,768]{2,1,0:T(8,128)(2,1)}, bf16[4,96,768]{2,1,0:T(8,128)(2,1)S(1)}, u32[]{:S(2)}, u32[]{:S(2)}) collective-permute-start(bf16[4,96,768]{2,1,0:T(8,128)(2,1)} %get-tuple-element.319), channel_id=1, source_target_pairs={{0,4},{4,0},{8,12},{12,8},{16,20},{20,16},{24,28},{28,24},{1,5},{5... | collective-permute-start | bytes 1769480 | tf_op jit(solution)/shard_map/ppermute | solution.py:1246
  (82 other events, 586.2 us)
where the time goes:
time: 479 us; the launch traced here: 473 us
  Pallas kernels  326 us (68%)
  waiting for transfers between devices  79.2 us (17%)
  starting transfers between devices  46.8 us (10%)
  local copies, waits for them, and re-layouts  18 us (4%)
    pallas_call x20, Pallas kernels, run(): pl.pallas_call(kernel, out_shape=[outs[n] for n in out_names] + [small_ou...  260 us
    ppermute x24, waiting for transfers between devices, dp_hop(): return lax.ppermute(values, 'dp', [(i, i ^ step) for i in range(size)])  50.4 us
    pallas_call x8, Pallas kernels, advance(): pl.pallas_call(partial(merge_kernel, spots=spots, after=len(after)), grid...  34.4 us
    ppermute x45, waiting for transfers between devices, tensor_hop(): return lax.ppermute(values, 'tensor', [(i, i ^ step) for i in range(4)])  28.7 us
    ppermute x24, starting transfers between devices, dp_hop(): return lax.ppermute(values, 'dp', [(i, i ^ step) for i in range(size)])  27.9 us
    pallas_call x8, Pallas kernels, plain(): pl.pallas_call(lambda *refs: body(*refs[:first], *refs[first + len(after)...  22.4 us
    ppermute x45, starting transfers between devices, tensor_hop(): return lax.ppermute(values, 'tensor', [(i, i ^ step) for i in range(4)])  19 us
    unnamed x75, local copies, waits for them, and re-layouts  13.7 us
  transfers between devices with their start and end apart: 69, of which 29 were waited for; matrix products, arithmetic and copies ran while one was open for 1% of the time, Pallas kernels for 55%

commit v1 on v0

--- a/solution.py
+++ b/solution.py
@@ -18,7 +18,7 @@
 SLOTS = WINDOW // UNIT
 FAR = -1e30
 SIDES = ("send", "keep")
-VMEM_BYTES = 66_000_000
+VMEM_BYTES = 66_600_000
 BF = jnp.bfloat16
 F32 = jnp.float32
 ROOT = math.sqrt(2.0 / math.pi)
@@ -1482,10 +1482,12 @@
             kept[-1]["branch3"] = branch3
         kv_sib = tensor_hop(kv, 1)
         opened = (
-            open_gate([entry1], [2, 3], [], [], [(over_x, 1)])
+            open_gate([entry1], [2, 3, 4], [], [], [(over_x, 1)])
             if layer == 0
-            else open_gate([entry1], [5], [], [], [(over_x, 4), (over_y, 3)])
+            else open_gate([entry1], [5], [], [3], [(over_x, 3), (sibs, 3)])
         )
+        if layer == 0:
+            end(1)
         (q,) = run(
             q_kernel,
             "query",
@@ -1499,51 +1501,89 @@
             [],
             15.0,
         )
-        x1, mixed1, rest1, lse1, branch1 = run(
-            self_kernel,
-            "self",
-            info,
-            dict(q=q, kv_own=kv, kv_sib=kv_sib, x=x),
-            dict(mod=mod, bias=(out_biases[0], (layer,))),
-            weights_of(first),
-            dict(out=frame_high, mixed=frame_low, rest=frame_low, lse=logs, branch=frame_low),
-            {},
-            dict(wo=whole, logs=log_work, sum=floats, sems=sems(4)),
-            opened,
-            8.0,
-        )
         if layer == 0:
-            opened = open_gate([x1], [4], [2], [1], [(along_x, 3)])
+            x1, mixed1, rest1, lse1, branch1, x2, entry2, cq, ckv, mixed2, lse2, branch2 = run(
+                lambda info, work, w: attention_kernel(info, work, w, words),
+                "self_cross",
+                info,
+                dict(q=q, kv_own=kv, kv_sib=kv_sib, x=x, text=text_rows),
+                dict(
+                    mod=mod,
+                    biases=biases,
+                    self_bias=(out_biases[0], (layer,)),
+                    cross_bias=(out_biases[1], (layer,)),
+                ),
+                weights_of(first) + weights_of(first + 1),
+                dict(
+                    x1=frame_high,
+                    mixed1=frame_low,
+                    rest=frame_low,
+                    lse1=logs,
+                    branch1=frame_low,
+                    out=frame_high,
+                    entry=frame_low,
+                    cq=frame_low,
+                    ckv=two_text,
+                    mixed2=frame_low,
+                    lse2=logs,
+                    branch2=frame_low,
+                ),
+                {},
+                dict(
+                    wq=whole,
+                    wk=whole,
+                    wv=whole,
+                    wo=whole,
+                    cross_wo=whole,
+                    logs=log_work,
+                    sum=floats,
+                    sems=sems(4),
+                    csems=sems(16),
+                ),
+                opened,
+                14.0,
+            )
+            opened = open_gate([x2], [], [2, 3], [], [(along_x, 4)])
             swap(2)
-        else:
-            opened = open_gate([x1], [], [5], [4])
-        x2, entry2, cq, ckv, mixed2, lse2, branch2 = run(
-            partial(cross_kernel, words=words),
-            "cross",
-            info,
-            dict(x=x1, text=text_rows),
-            dict(mod=mod, biases=biases, bias=(out_biases[1], (layer,))),
-            weights_of(first + 1),
-            dict(
-                out=frame_high,
-                entry=frame_low,
-                q=frame_low,
-                kv=two_text,
-                mixed=frame_low,
-                lse=logs,
-                branch=frame_low,
-            ),
-            {},
-            dict(
-                wq=whole, wk=whole, wv=whole, wo=whole, logs=log_work, sum=floats, sems=sems(16)
-            ),
-            opened,
-            6.0,
-        )
-        if layer == 0:
-            opened = open_gate([x2], [], [3], [2], [(over_x, 2), (sibs, 2), (along_x, 4)])
             swap(3)
         else:
+            x1, mixed1, rest1, lse1, branch1 = run(
+                self_kernel,
+                "self",
+                info,
+                dict(q=q, kv_own=kv, kv_sib=kv_sib, x=x),
+                dict(mod=mod, bias=(out_biases[0], (layer,))),
+                weights_of(first),
+                dict(out=frame_high, mixed=frame_low, rest=frame_low, lse=logs, branch=frame_low),
+                {},
+                dict(wo=whole, logs=log_work, sum=floats, sems=sems(4)),
+                opened,
+                8.0,
+            )
+            opened = open_gate([x1], [], [5], [4], [(over_x, 4), (over_y, 3)])
+            x2, entry2, cq, ckv, mixed2, lse2, branch2 = run(
+                partial(cross_kernel, words=words),
+                "cross",
+                info,
+                dict(x=x1, text=text_rows),
+                dict(mod=mod, biases=biases, bias=(out_biases[1], (layer,))),
+                weights_of(first + 1),
+                dict(
+                    out=frame_high,
+                    entry=frame_low,
+                    q=frame_low,
+                    kv=two_text,
+                    mixed=frame_low,
+                    lse=logs,
+                    branch=frame_low,
+                ),
+                {},
+                dict(
+                    wq=whole, wk=whole, wv=whole, wo=whole, logs=log_work, sum=floats, sems=sems(16)
+                ),
+                opened,
+                6.0,
+            )
             opened = open_gate([x2], [], [], [5], [(over_x, 5), (over_y, 4)])
         if layer == 0:
             part, entry3, active, slope = run(
@@ -1561,7 +1601,7 @@
                 opened,
                 5.0,
             )
-            opened = open_gate([part], [], [4], [3], [(over_x, 3), (over_y, 2), (sibs, 3)])
+            opened = open_gate([part], [], [4], [2], [(over_x, 2), (sibs, 2)])
             x3 = branch3 = None
         else:
             x3 = branch3 = active = slope = entry3 = None

time: 479 us -> 486 us (1.015)
  waiting for transfers between devices: 79.2 us -> 97.4 us
  local copies, waits for them, and re-layouts: 18 us -> 10.9 us
    ppermute x45, waiting for transfers between devices: 28.7 us -> 39.2 us  [tensor_hop(): return lax.ppermute(values, 'tensor', [(i, i ^ step) for i in range(4)])]
    ppermute x24, waiting for transfers between devices: 50.4 us -> 58.3 us  [dp_hop(): return lax.ppermute(values, 'dp', [(i, i ^ step) for i in range(size)])]
    unnamed x75 -> x37, local copies, waits for them, and re-layouts: 13.7 us -> 5.96 us
    pallas_call x20 -> x19, Pallas kernels: 260 us -> 256 us  [run(): pl.pallas_call(kernel, out_shape=[outs[n] for n in out_names] + [small_ou...]
  transfers between devices with their start and end apart: 69 -> 69, of which waited for: 29 -> 29; matrix products, arithmetic and copies ran while one was open for 1% -> 2% of each run, Pallas kernels for 55% -> 56%
where the time goes in v1:
time: 486 us; the launch traced here: 480 us
  Pallas kernels  322 us (66%)
  waiting for transfers between devices  97.4 us (20%)
  starting transfers between devices  45.9 us (9%)
  local copies, waits for them, and re-layouts  10.9 us (2%)
    pallas_call x19, Pallas kernels, run(): pl.pallas_call(kernel, out_shape=[outs[n] for n in out_names] + [small_ou...  256 us
    ppermute x24, waiting for transfers between devices, dp_hop(): return lax.ppermute(values, 'dp', [(i, i ^ step) for i in range(size)])  58.3 us
    ppermute x45, waiting for transfers between devices, tensor_hop(): return lax.ppermute(values, 'tensor', [(i, i ^ step) for i in range(4)])  39.2 us
    pallas_call x8, Pallas kernels, advance(): pl.pallas_call(partial(merge_kernel, spots=spots, after=len(after)), grid...  34.4 us
    ppermute x24, starting transfers between devices, dp_hop(): return lax.ppermute(values, 'dp', [(i, i ^ step) for i in range(size)])  26.1 us
    pallas_call x8, Pallas kernels, plain(): pl.pallas_call(lambda *refs: body(*refs[:first], *refs[first + len(after)...  22.4 us
    ppermute x45, starting transfers between devices, tensor_hop(): return lax.ppermute(values, 'tensor', [(i, i ^ step) for i in range(4)])  19.8 us
  transfers between devices with their start and end apart: 69, of which 29 were waited for; matrix products, arithmetic and copies ran while one was open for 2% of the time, Pallas kernels for 56%

profile of v1, /device:TPU:0, one launch (start us, length us, event | category | flops | bytes accessed | tf_op | source)
XLA Modules:
  0.0 480.4 jit_solution(9615730206291485907)
XLA Ops:
  16.8 5.8 %pack_weights.2 = (bf16[768,768]{1,0:T(8,128)(2,1)}, bf16[768,768]{1,0:T(8,128)(2,1)}, bf16[768,768]{1,0:T(8,128)(2,1)}, bf16[384,768]{1,0:T(8,128)(2,1)}, bf16[...) custom-call(s32[9]{0:T(128)} %concatenate.6.info.refs_0_, ...), custom_call_target="tpu_custom_call" | custom-call | flops 400000000 | bytes 1000 | tf_op jit(solution)/shard_map/pack_weights/pallas_call | solution.py:1309
  29.3 9.0 %collective-permute-done.6.refs_0_ = bf16[384,768]{1,0:T(8,128)(2,1)} collective-permute-done((bf16[384,768]{1,0:T(8,128)(2,1)}, bf16[384,768]{1,0:T(8,128)(2,1)}, u32[]{:S(2)}, u32[]{:S(2)}) %collective-permute-start.6) | collective-permute-done | bytes 589856 | tf_op jit(solution)/shard_map/ppermute | solution.py:1246
  47.1 6.6 %self_kv.1 = (bf16[512,768]{1,0:T(8,128)(2,1)}, bf16[2,512,768]{2,1,0:T(8,128)(2,1)}, f32[512,768]{1,0:T(8,128)}) custom-call(s32[9]{0:T(128)} %concatenate.6.info.refs_0_, f32[2,4,6912]{2,1,0:T(4,128)} %get-tuple-element.185.refs_1_.refs_6_.refs_2_.refs_4_.refs_5_.refs_3_.refs_10_.refs_9_.refs_7_.refs_13_, ...), custom_call_target="tpu_custom_call" | custom-call | flops 1200000000 | bytes 1000 | tf_op jit(solution)/shard_map/self_kv/pallas_call | solution.py:162
  54.3 6.5 %collective-permute-done.13.refs_19_.refs_18_ = bf16[384,768]{1,0:T(8,128)(2,1)} collective-permute-done((bf16[384,768]{1,0:T(8,128)(2,1)}, bf16[384,768]{1,0:T(8,128)(2,1)}, u32[]{:S(2)}, u32[]{:S(2)}) %collective-permute-start.13) | collective-permute-done | bytes 589856 | tf_op jit(solution)/shard_map/ppermute | solution.py:1246
  73.1 26.9 %self_cross.1 = (f32[512,768]{1,0:T(8,128)}, bf16[512,768]{1,0:T(8,128)(2,1)}, bf16[512,768]{1,0:T(8,128)(2,1)}, f32[16,512]{1,0:T(8,128)}, bf16[512,768]{1,0:T(...) custom-call(s32[9]{0:T(128)} %concatenate.6.info.refs_0_, ...), custom_call_target="tpu_custom_call" | custom-call | flops 5600000000 | bytes 1000 | tf_op jit(solution)/shard_map/self_cross/pallas_call | solution.py:162
  100.1 6.1 %collective-permute-done.18.refs_2_ = bf16[384,768]{1,0:T(8,128)(2,1)} collective-permute-done((bf16[384,768]{1,0:T(8,128)(2,1)}, bf16[384,768]{1,0:T(8,128)(2,1)}, u32[]{:S(2)}, u32[]{:S(2)}) %collective-permute-start.18) | collective-permute-done | bytes 589856 | tf_op jit(solution)/shard_map/ppermute | solution.py:1241
  107.6 9.8 %ff_part.1 = (bf16[512,768]{1,0:T(8,128)(2,1)}, bf16[512,768]{1,0:T(8,128)(2,1)}, bf16[512,1536]{1,0:T(8,128)(2,1)}, bf16[512,1536]{1,0:T(8,128)(2,1)}) custom-call(s32[9]{0:T(128)} %concatenate.6.info.refs_0_, f32[512,768]{1,0:T(8,128)} %get-tuple-element.199.refs_3_.refs_1_.refs_12_, ...), custom_call_target="tpu_custom_call" | custom-call | flops 2000000000 | bytes 1000 | tf_op jit(solution)/shard_map/ff_part/pallas_call | solution.py:162
  123.3 14.2 %collective-permute-done.19.refs_2_ = bf16[512,768]{1,0:T(8,128)(2,1)} collective-permute-done((bf16[512,768]{1,0:T(8,128)(2,1)}, bf16[512,768]{1,0:T(8,128)(2,1)}, u32[]{:S(2)}, u32[]{:S(2)}) %collective-permute-start.19) | collective-permute-done | bytes 786464 | tf_op jit(solution)/shard_map/ppermute | solution.py:1241
  137.5 7.9 %residual_kv.1 = (bf16[512,768]{1,0:T(8,128)(2,1)}, bf16[2,512,768]{2,1,0:T(8,128)(2,1)}, f32[512,768]{1,0:T(8,128)}, bf16[512,768]{1,0:T(8,128)(2,1)}) custom-call(s32[9]{0:T(128)} %concatenate.6.info.refs_0_, bf16[512,768]{1,0:T(8,128)(2,1)} %get-tuple-element.204.refs_4_.refs_1_, bf16[512,768]{1,0:T(8,128)(2,1)} %collective-permute-done.19.refs_2_, ...), custom_call_target="tpu_custom_call" | custom-call | flops 1200000000 | bytes 1000 | tf_op jit(solution)/shard_map/residual_kv/pallas_call | solution.py:162
  150.4 12.0 %collective-permute-done.25.refs_1_ = bf16[384,768]{1,0:T(8,128)(2,1)S(1)} collective-permute-done((bf16[384,768]{1,0:T(8,128)(2,1)}, bf16[384,768]{1,0:T(8,128)(2,1)S(1)}, u32[]{:S(2)}, u32[]{:S(2)}) %collective-permute-start.25) | collective-permute-done | bytes 589856 | tf_op jit(solution)/shard_map/ppermute | solution.py:1246
  169.1 17.1 %self.1 = (f32[512,768]{1,0:T(8,128)}, bf16[512,768]{1,0:T(8,128)(2,1)}, bf16[512,768]{1,0:T(8,128)(2,1)}, f32[16,512]{1,0:T(8,128)}, bf16[512,768]{1,0:T(8,128)(2,1)}) custom-call(s32[9]{0:T(128)} %concatenate.6.info.refs_0_, bf16[512,768]{1,0:T(8,128)(2,1)} %query.3.refs_1_.refs_5_, bf16[2,512,768]{2,1,0:T(8,128)(2,1)} %get-tuple-element.211.refs_2_.refs_6_, ...), custom_call_target="tpu_custom_call" | custom-call | flops 3200000000 | bytes 1000 | tf_op jit(solution)/shard_map/self/pallas_call | solution.py:162
  187.4 14.2 %cross.1 = (f32[512,768]{1,0:T(8,128)}, bf16[512,768]{1,0:T(8,128)(2,1)}, bf16[512,768]{1,0:T(8,128)(2,1)}, bf16[2,512,768]{2,1,0:T(8,128)(2,1)}, bf16[512,768]{...) custom-call(s32[9]{0:T(128)} %concatenate.6.info.refs_0_, ...), custom_call_target="tpu_custom_call" | custom-call | flops 2400000000 | bytes 1000 | tf_op jit(solution)/shard_map/cross/pallas_call | solution.py:162
  205.2 37.4 %ff_cross_back.1 = (bf16[768,1536]{1,0:T(8,128)(2,1)}, bf16[768,1536]{1,0:T(8,128)(2,1)}, bf16[512,768]{1,0:T(8,128)(2,1)}, bf16[768,768]{1,0:T(8,128)(2,1)}, bf...) custom-call(s32[9]{0:T(128)} %concatenate.6.info.refs_0_, ...), custom_call_target="tpu_custom_call" | custom-call | flops 4000000000 | bytes 1000 | tf_op jit(solution)/shard_map/ff_cross_back/pallas_call | solution.py:162
  243.3 26.1 %self_back.2 = (bf16[512,768]{1,0:T(8,128)(2,1)}, bf16[512,768]{1,0:T(8,128)(2,1)}, bf16[2,512,768]{2,1,0:T(8,128)(2,1)}, bf16[2,512,768]{2,1,0:T(8,128)(2,1)}, f32[72,768]{1,0:T(8,128)}) custom-call(s32[9]{0:T(128)} %concatenate.6.info.refs_0_, f32[512,768]{1,0:T(8,128)} %get-tuple-element.235.refs_1_.refs_6_, bf16[512,768]{1,0:T(8,128)(2,1)} %get-tuple-element.236.refs_2_, ...), custom_call_target="tpu_custom_call" | custom-call | flops 5200000000 | bytes 1000 | tf_op jit(solution)/shard_map/self_back/pallas_call | solution.py:162
  280.2 12.4 %qkv_back.2 = (bf16[768,384]{1,0:T(8,128)(2,1)}, bf16[768,384]{1,0:T(8,128)(2,1)}, f32[512,768]{1,0:T(8,128)}, f32[72,768]{1,0:T(8,128)}) custom-call(s32[9]{0:T(128)} %concatenate.6.info.refs_0_, bf16[2,512,768]{2,1,0:T(8,128)(2,1)} %get-tuple-element.243.refs_1_, bf16[2,512,768]{2,1,0:T(8,128)(2,1)} %collective-permute-done.37.refs_2_, ...), custom_call_target="tpu_custom_call" | custom-call | flops 2400000000 | bytes 1000 | tf_op jit(solution)/shard_map/qkv_back/pallas_call | solution.py:162
  295.8 7.1 %collective-permute-done.39 = bf16[4,96,1536]{2,1,0:T(8,128)(2,1)} collective-permute-done((bf16[4,96,1536]{2,1,0:T(8,128)(2,1)}, bf16[4,96,1536]{2,1,0:T(8,128)(2,1)}, u32[]{:S(2)}, u32[]{:S(2)}) %collective-permute-start.39) | collective-permute-done | bytes 1179680 | tf_op jit(solution)/shard_map/ppermute | solution.py:1246
  302.9 5.9 %merge_grads.9 = (bf16[2,96,1536]{2,1,0:T(8,128)(2,1)}, bf16[2,96,1536]{2,1,0:T(8,128)(2,1)}, bf16[4,96,1536]{2,1,0:T(8,128)(2,1)}, bf16[4,96,1536]{2,1,0:T(8,128)(2,1)}) custom-call(s32[9]{0:T(128)} %concatenate.6.info.refs_0_, bf16[2,2,96,1536]{3,2,1,0:T(8,128)(2,1)} %bitcast.21.refs_0_.refs_2_, bf16[2,2,96,1536]{3,2,1,0:T(8,128)(2,1)} %bitcast.83, ...), custom_call_target="tpu_custom_call" | custom-call | flops 600000000 | bytes 1000 | tf_op jit(solution)/shard_map/merge_grads/pallas_call | solution.py:1682
  309.5 10.8 %ff_back.1 = (bf16[512,768]{1,0:T(8,128)(2,1)}, bf16[512,768]{1,0:T(8,128)(2,1)}, bf16[512,1536]{1,0:T(8,128)(2,1)}, f32[72,768]{1,0:T(8,128)}) custom-call(s32[9]{0:T(128)} %concatenate.6.info.refs_0_, f32[512,768]{1,0:T(8,128)} %get-tuple-element.251.refs_16_.refs_1_, bf16[512,768]{1,0:T(8,128)(2,1)} %get-tuple-element.252.refs_2_, ...), custom_call_target="tpu_custom_call" | custom-call | flops 2000000000 | bytes 1000 | tf_op jit(solution)/shard_map/ff_back/pallas_call | solution.py:162
  324.0 7.4 %ff_grads.1 = (bf16[768,1536]{1,0:T(8,128)(2,1)}, bf16[768,1536]{1,0:T(8,128)(2,1)}) custom-call(s32[9]{0:T(128)} %concatenate.6.info.refs_0_, bf16[512,768]{1,0:T(8,128)(2,1)} %get-tuple-element.271.refs_1_, bf16[512,1536]{1,0:T(8,128)(2,1)} %get-tuple-element.272.refs_2_, bf16[512,768]{1,0:T(8,128)(2,1)} %get-tuple-element.261.refs_3_.refs_5_, ...), custom_call_target="tpu_custom_call" | custom-call | flops 400000000 | bytes 1000 | tf_op jit(solution)/shard_map/ff_grads/pallas_call | solution.py:162
  346.4 19.3 %cross_back.1 = (bf16[768,768]{1,0:T(8,128)(2,1)}, bf16[768,768]{1,0:T(8,128)(2,1)}, f32[512,768]{1,0:T(8,128)}, f32[72,768]{1,0:T(8,128)}) custom-call(s32[9]{0:T(128)} %concatenate.6.info.refs_0_, f32[512,768]{1,0:T(8,128)} %get-tuple-element.251.refs_16_.refs_1_, bf16[512,768]{1,0:T(8,128)(2,1)} %get-tuple-element.262.refs_2_, ...), custom_call_target="tpu_custom_call" | custom-call | flops 24000000000 | bytes 1000 | tf_op jit(solution)/shard_map/cross_back/pallas_call | solution.py:162
  366.5 5.2 %merge_grads.11 = (bf16[4,96,1536]{2,1,0:T(8,128)(2,1)}, bf16[4,96,1536]{2,1,0:T(8,128)(2,1)}, bf16[1,96,1536]{2,1,0:T(8,128)(2,1)}, bf16[1,96,1536]{2,1,0:T(8,128)(2,1)}) custom-call(s32[9]{0:T(128)} %concatenate.6.info.refs_0_, bf16[4,2,96,1536]{3,2,1,0:T(8,128)(2,1)} %bitcast.34.refs_0_.refs_2_, bf16[4,2,96,1536]{3,2,1,0:T(8,128)(2,1)} %bitcast.74, ...), custom_call_target="tpu_custom_call" | custom-call | flops 600000000 | bytes 1000 | tf_op jit(solution)/shard_map/merge_grads/pallas_call | solution.py:1682
  372.3 26.2 %self_back.3 = (bf16[512,768]{1,0:T(8,128)(2,1)}, bf16[512,768]{1,0:T(8,128)(2,1)}, bf16[2,512,768]{2,1,0:T(8,128)(2,1)}, bf16[2,512,768]{2,1,0:T(8,128)(2,1)}, f32[72,768]{1,0:T(8,128)}) custom-call(s32[9]{0:T(128)} %concatenate.6.info.refs_0_, f32[512,768]{1,0:T(8,128)} %get-tuple-element.279.refs_8_.refs_1_.refs_4_, ...), custom_call_target="tpu_custom_call" | custom-call | flops 5200000000 | bytes 1000 | tf_op jit(solution)/shard_map/self_back/pallas_call | solution.py:162
  411.5 5.8 %kv_grads.1 = (bf16[768,384]{1,0:T(8,128)(2,1)}, bf16[768,384]{1,0:T(8,128)(2,1)}, bf16[2,512,768]{2,1,0:T(8,128)(2,1)}) custom-call(s32[9]{0:T(128)} %concatenate.6.info.refs_0_, bf16[2,512,768]{2,1,0:T(8,128)(2,1)} %get-tuple-element.291.refs_1_, bf16[2,512,768]{2,1,0:T(8,128)(2,1)} %collective-permute-done.49.refs_2_, ...), custom_call_target="tpu_custom_call" | custom-call | flops 1600000000 | bytes 1000 | tf_op jit(solution)/shard_map/kv_grads/pallas_call | solution.py:162
  430.4 9.6 %qkv_back.3 = (bf16[512,768]{1,0:T(8,128)(2,1)}, f32[512,768]{1,0:T(8,128)}, f32[72,768]{1,0:T(8,128)}) custom-call(s32[9]{0:T(128)} %concatenate.6.info.refs_0_, bf16[2,512,768]{2,1,0:T(8,128)(2,1)} %get-tuple-element.301.refs_1_, bf16[512,768]{1,0:T(8,128)(2,1)} %get-tuple-element.294.refs_8_.refs_3_.refs_2_, ...), custom_call_target="tpu_custom_call" | custom-call | flops 2400000000 | bytes 1000 | tf_op jit(solution)/shard_map/qkv_back/pallas_call | solution.py:162
  (215 shorter events, 169.7 us)
Async XLA Ops:
  8.4 38.6 %collective-permute-start.10 = (bf16[2,768,768]{2,1,0:T(8,128)(2,1)}, bf16[2,768,768]{2,1,0:T(8,128)(2,1)}, u32[]{:S(2)}, u32[]{:S(2)}) collective-permute-start(bf16[2,768,768]{2,1,0:T(8,128)(2,1)} %refs_5_.3), channel_id=1, source_target_pairs={{0,1},{1,0},{2,3},{3,2},{4,5},{5,4},{6,7},{7,6},{8,9},{9,8},{10,11... | collective-permute-start | bytes 7077896 | tf_op jit(solution)/shard_map/ppermute | solution.py:1241
  8.4 38.6 %collective-permute-start.11 = (bf16[2,768,768]{2,1,0:T(8,128)(2,1)}, bf16[2,768,768]{2,1,0:T(8,128)(2,1)}, u32[]{:S(2)}, u32[]{:S(2)}) collective-permute-start(bf16[2,768,768]{2,1,0:T(8,128)(2,1)} %refs_7_.5), channel_id=1, source_target_pairs={{0,1},{1,0},{2,3},{3,2},{4,5},{5,4},{6,7},{7,6},{8,9},{9,8},{10,11... | collective-permute-start | bytes 7077896 | tf_op jit(solution)/shard_map/ppermute | solution.py:1241
  60.8 58.3 %collective-permute-start.22 = (bf16[768,768]{1,0:T(8,128)(2,1)}, bf16[768,768]{1,0:T(8,128)(2,1)}, u32[]{:S(2)}, u32[]{:S(2)}) collective-permute-start(bf16[768,768]{1,0:T(8,128)(2,1)} %get-tuple-element.205.refs_8_.refs_3_.refs_7_.refs_11_.refs_9_), channel_id=1, source_target_pairs={{0,1},{1,0},{2,3},{3,2},{4,5},{5,4},{6,7},{7,6},{8,9},{9,8},{10,11... | collective-permute-start | bytes 3538952 | tf_op jit(solution)/shard_map/ppermute | solution.py:1241
  65.3 34.7 %collective-permute-start.16 = (bf16[384,768]{1,0:T(8,128)(2,1)}, bf16[384,768]{1,0:T(8,128)(2,1)}, u32[]{:S(2)}, u32[]{:S(2)}) collective-permute-start(bf16[384,768]{1,0:T(8,128)(2,1)} %get-tuple-element.196.refs_22_), channel_id=1, source_target_pairs={{0,2},{1,3},{2,0},{3,1},{4,6},{5,7},{6,4},{7,5},{8,10},{9,11},{10,... | collective-permute-start | bytes 1769480 | tf_op jit(solution)/shard_map/ppermute | solution.py:1241
  66.8 33.3 %collective-permute-start.17 = (bf16[384,768]{1,0:T(8,128)(2,1)}, bf16[384,768]{1,0:T(8,128)(2,1)}, u32[]{:S(2)}, u32[]{:S(2)}) collective-permute-start(bf16[384,768]{1,0:T(8,128)(2,1)} %get-tuple-element.197.refs_23_), channel_id=1, source_target_pairs={{0,2},{1,3},{2,0},{3,1},{4,6},{5,7},{6,4},{7,5},{8,10},{9,11},{10,... | collective-permute-start | bytes 1769480 | tf_op jit(solution)/shard_map/ppermute | solution.py:1241
  67.4 38.8 %collective-permute-start.18 = (bf16[384,768]{1,0:T(8,128)(2,1)}, bf16[384,768]{1,0:T(8,128)(2,1)}, u32[]{:S(2)}, u32[]{:S(2)}) collective-permute-start(bf16[384,768]{1,0:T(8,128)(2,1)} %get-tuple-element.198.refs_24_), channel_id=1, source_target_pairs={{0,2},{1,3},{2,0},{3,1},{4,6},{5,7},{6,4},{7,5},{8,10},{9,11},{10,... | collective-permute-start | bytes 1769480 | tf_op jit(solution)/shard_map/ppermute | solution.py:1241
  122.2 24.3 %collective-permute-start.27 = (bf16[768,768]{1,0:T(8,128)(2,1)}, bf16[768,768]{1,0:T(8,128)(2,1)}, u32[]{:S(2)}, u32[]{:S(2)}) collective-permute-start(bf16[768,768]{1,0:T(8,128)(2,1)} %get-tuple-element.214.refs_6_.refs_26_), channel_id=1, source_target_pairs={{0,1},{1,0},{2,3},{3,2},{4,5},{5,4},{6,7},{7,6},{8,9},{9,8},{10,11... | collective-permute-start | bytes 3538952 | tf_op jit(solution)/shard_map/ppermute | solution.py:1241
  145.4 23.7 %collective-permute-start.24 = (bf16[2,512,768]{2,1,0:T(8,128)(2,1)}, bf16[2,512,768]{2,1,0:T(8,128)(2,1)}, u32[]{:S(2)}, u32[]{:S(2)}) collective-permute-start(bf16[2,512,768]{2,1,0:T(8,128)(2,1)} %get-tuple-element.211.refs_2_.refs_6_), channel_id=1, source_target_pairs={{0,1},{1,0},{2,3},{3,2},{4,5},{5,4},{6,7},{7,6},{8,9},{9,8},{10,11... | collective-permute-start | bytes 4718600 | tf_op jit(solution)/shard_map/ppermute | solution.py:1241
  146.6 39.6 %collective-permute-start.30 = (bf16[384,768]{1,0:T(8,128)(2,1)}, bf16[384,768]{1,0:T(8,128)(2,1)}, u32[]{:S(2)}, u32[]{:S(2)}) collective-permute-start(bf16[384,768]{1,0:T(8,128)(2,1)} %get-tuple-element.209.refs_14_.refs_15_), channel_id=1, source_target_pairs={{0,1},{1,0},{2,3},{3,2},{4,5},{5,4},{6,7},{7,6},{8,9},{9,8},{10,11... | collective-permute-start | bytes 1769480 | tf_op jit(solution)/shard_map/ppermute | solution.py:1241
  146.6 39.6 %collective-permute-start.29 = (bf16[384,768]{1,0:T(8,128)(2,1)}, bf16[384,768]{1,0:T(8,128)(2,1)}, u32[]{:S(2)}, u32[]{:S(2)}) collective-permute-start(bf16[384,768]{1,0:T(8,128)(2,1)} %get-tuple-element.209.refs_14_.refs_15_), channel_id=1, source_target_pairs={{0,4},{4,0},{8,12},{12,8},{16,20},{20,16},{24,28},{28,24},{1,5},{5... | collective-permute-start | bytes 1769480 | tf_op jit(solution)/shard_map/ppermute | solution.py:1246
  163.2 23.0 %collective-permute-start.28 = (bf16[384,768]{1,0:T(8,128)(2,1)}, bf16[384,768]{1,0:T(8,128)(2,1)}, u32[]{:S(2)}, u32[]{:S(2)}) collective-permute-start(bf16[384,768]{1,0:T(8,128)(2,1)} %get-tuple-element.215.refs_13_), channel_id=1, source_target_pairs={{0,2},{1,3},{2,0},{3,1},{4,6},{5,7},{6,4},{7,5},{8,10},{9,11},{10,... | collective-permute-start | bytes 1769480 | tf_op jit(solution)/shard_map/ppermute | solution.py:1241
  164.7 21.5 %collective-permute-start.31 = (bf16[384,768]{1,0:T(8,128)(2,1)}, bf16[384,768]{1,0:T(8,128)(2,1)}, u32[]{:S(2)}, u32[]{:S(2)}) collective-permute-start(bf16[384,768]{1,0:T(8,128)(2,1)} %get-tuple-element.216.refs_14_.refs_9_.refs_29_), channel_id=1, source_target_pairs={{0,1},{1,0},{2,3},{3,2},{4,5},{5,4},{6,7},{7,6},{8,9},{9,8},{10,11... | collective-permute-start | bytes 1769480 | tf_op jit(solution)/shard_map/ppermute | solution.py:1241
  242.6 27.3 %collective-permute-start.38 = (bf16[768,1536]{1,0:T(8,128)(2,1)}, bf16[768,1536]{1,0:T(8,128)(2,1)}, u32[]{:S(2)}, u32[]{:S(2)}) collective-permute-start(bf16[768,1536]{1,0:T(8,128)(2,1)} %get-tuple-element.247), channel_id=1, source_target_pairs={{0,1},{1,0},{2,3},{3,2},{4,5},{5,4},{6,7},{7,6},{8,9},{9,8},{10,11... | collective-permute-start | bytes 7077896 | tf_op jit(solution)/shard_map/ppermute | solution.py:1241
  243.2 49.9 %collective-permute-start.40 = (bf16[768,768]{1,0:T(8,128)(2,1)}, bf16[768,768]{1,0:T(8,128)(2,1)}, u32[]{:S(2)}, u32[]{:S(2)}) collective-permute-start(bf16[768,768]{1,0:T(8,128)(2,1)} %get-tuple-element.255), channel_id=1, source_target_pairs={{0,1},{1,0},{2,3},{3,2},{4,5},{5,4},{6,7},{7,6},{8,9},{9,8},{10,11... | collective-permute-start | bytes 3538952 | tf_op jit(solution)/shard_map/ppermute | solution.py:1241
  274.7 28.3 %collective-permute-start.39 = (bf16[4,96,1536]{2,1,0:T(8,128)(2,1)}, bf16[4,96,1536]{2,1,0:T(8,128)(2,1)}, u32[]{:S(2)}, u32[]{:S(2)}) collective-permute-start(bf16[4,96,1536]{2,1,0:T(8,128)(2,1)} %get-tuple-element.254), channel_id=1, source_target_pairs={{0,4},{4,0},{8,12},{12,8},{16,20},{20,16},{24,28},{28,24},{1,5},{5... | collective-permute-start | bytes 3538952 | tf_op jit(solution)/shard_map/ppermute | solution.py:1246
  308.8 29.5 %collective-permute-start.45 = (bf16[4,96,1536]{2,1,0:T(8,128)(2,1)}, bf16[4,96,1536]{2,1,0:T(8,128)(2,1)}, u32[]{:S(2)}, u32[]{:S(2)}) collective-permute-start(bf16[4,96,1536]{2,1,0:T(8,128)(2,1)} %get-tuple-element.276), channel_id=1, source_target_pairs={{0,4},{4,0},{8,12},{12,8},{16,20},{20,16},{24,28},{28,24},{1,5},{5... | collective-permute-start | bytes 3538952 | tf_op jit(solution)/shard_map/ppermute | solution.py:1246
  309.5 21.9 %collective-permute-start.36 = (bf16[512,768]{1,0:T(8,128)(2,1)}, bf16[512,768]{1,0:T(8,128)(2,1)}, u32[]{:S(2)}, u32[]{:S(2)}) collective-permute-start(bf16[512,768]{1,0:T(8,128)(2,1)} %get-tuple-element.234.refs_1_), channel_id=1, source_target_pairs={{0,1},{1,0},{2,3},{3,2},{4,5},{5,4},{6,7},{7,6},{8,9},{9,8},{10,11... | collective-permute-start | bytes 2359304 | tf_op jit(solution)/shard_map/ppermute | solution.py:1241
  320.4 26.0 %collective-permute-start.43 = (bf16[512,768]{1,0:T(8,128)(2,1)}, bf16[512,768]{1,0:T(8,128)(2,1)}, u32[]{:S(2)}, u32[]{:S(2)}) collective-permute-start(bf16[512,768]{1,0:T(8,128)(2,1)} %get-tuple-element.269.refs_10_), channel_id=1, source_target_pairs={{0,2},{1,3},{2,0},{3,1},{4,6},{5,7},{6,4},{7,5},{8,10},{9,11},{10,... | collective-permute-start | bytes 2359304 | tf_op jit(solution)/shard_map/ppermute | solution.py:1241
  331.4 34.4 %collective-permute-start.46 = (bf16[768,1536]{1,0:T(8,128)(2,1)}, bf16[768,1536]{1,0:T(8,128)(2,1)}, u32[]{:S(2)}, u32[]{:S(2)}) collective-permute-start(bf16[768,1536]{1,0:T(8,128)(2,1)} %get-tuple-element.285), channel_id=1, source_target_pairs={{0,1},{1,0},{2,3},{3,2},{4,5},{5,4},{6,7},{7,6},{8,9},{9,8},{10,11... | collective-permute-start | bytes 7077896 | tf_op jit(solution)/shard_map/ppermute | solution.py:1241
  342.3 23.5 %collective-permute-start.48 = (bf16[1,96,1536]{2,1,0:T(8,128)(2,1)}, bf16[1,96,1536]{2,1,0:T(8,128)(2,1)S(1)}, u32[]{:S(2)}, u32[]{:S(2)}) collective-permute-start(bf16[1,96,1536]{2,1,0:T(8,128)(2,1)} %get-tuple-element.287), channel_id=1, source_target_pairs={{0,16},{4,20},{8,24},{12,28},{16,0},{20,4},{24,8},{28,12},{1,17},{... | collective-permute-start | bytes 884744 | tf_op jit(solution)/shard_map/ppermute | solution.py:1246
  344.8 21.0 %collective-permute-start.47 = (bf16[2,96,1536]{2,1,0:T(8,128)(2,1)}, bf16[2,96,1536]{2,1,0:T(8,128)(2,1)}, u32[]{:S(2)}, u32[]{:S(2)}) collective-permute-start(bf16[2,96,1536]{2,1,0:T(8,128)(2,1)} %get-tuple-element.286), channel_id=1, source_target_pairs={{0,8},{4,12},{8,0},{12,4},{16,24},{20,28},{24,16},{28,20},{1,9},{5... | collective-permute-start | bytes 1769480 | tf_op jit(solution)/shard_map/ppermute | solution.py:1246
  365.7 32.9 %collective-permute-start.51 = (bf16[768,768]{1,0:T(8,128)(2,1)}, bf16[768,768]{1,0:T(8,128)(2,1)}, u32[]{:S(2)}, u32[]{:S(2)}) collective-permute-start(bf16[768,768]{1,0:T(8,128)(2,1)} %get-tuple-element.296), channel_id=1, source_target_pairs={{0,1},{1,0},{2,3},{3,2},{4,5},{5,4},{6,7},{7,6},{8,9},{9,8},{10,11... | collective-permute-start | bytes 3538952 | tf_op jit(solution)/shard_map/ppermute | solution.py:1241
  371.6 28.7 %collective-permute-start.50 = (bf16[4,96,1536]{2,1,0:T(8,128)(2,1)}, bf16[4,96,1536]{2,1,0:T(8,128)(2,1)}, u32[]{:S(2)}, u32[]{:S(2)}) collective-permute-start(bf16[4,96,1536]{2,1,0:T(8,128)(2,1)} %get-tuple-element.295), channel_id=1, source_target_pairs={{0,4},{4,0},{8,12},{12,8},{16,20},{20,16},{24,28},{28,24},{1,5},{5... | collective-permute-start | bytes 3538952 | tf_op jit(solution)/shard_map/ppermute | solution.py:1246
  371.9 26.6 %collective-permute-start.52 = (bf16[1,96,1536]{2,1,0:T(8,128)(2,1)}, bf16[1,96,1536]{2,1,0:T(8,128)(2,1)S(1)}, u32[]{:S(2)}, u32[]{:S(2)}) collective-permute-start(bf16[1,96,1536]{2,1,0:T(8,128)(2,1)} %get-tuple-element.297), channel_id=1, source_target_pairs={{0,16},{4,20},{8,24},{12,28},{16,0},{20,4},{24,8},{28,12},{1,17},{... | collective-permute-start | bytes 884744 | tf_op jit(solution)/shard_map/ppermute | solution.py:1246
  (63 other events, 592.1 us)

commit v2 on v1

--- a/solution.py
+++ b/solution.py
@@ -18,7 +18,7 @@
 SLOTS = WINDOW // UNIT
 FAR = -1e30
 SIDES = ("send", "keep")
-VMEM_BYTES = 66_600_000
+VMEM_BYTES = 66_000_000
 BF = jnp.bfloat16
 F32 = jnp.float32
 ROOT = math.sqrt(2.0 / math.pi)
@@ -1482,9 +1482,9 @@
             kept[-1]["branch3"] = branch3
         kv_sib = tensor_hop(kv, 1)
         opened = (
-            open_gate([entry1], [2, 3, 4], [], [], [(over_x, 1)])
+            open_gate([entry1], [2, 3, 4])
             if layer == 0
-            else open_gate([entry1], [5], [], [3], [(over_x, 3), (sibs, 3)])
+            else open_gate([entry1], [5], [], [], [(over_x, 3), (sibs, 3)])
         )
         if layer == 0:
             end(1)
@@ -1543,7 +1543,7 @@
                 opened,
                 14.0,
             )
-            opened = open_gate([x2], [], [2, 3], [], [(along_x, 4)])
+            opened = open_gate([x2], [], [2, 3])
             swap(2)
             swap(3)
         else:
@@ -1560,7 +1560,7 @@
                 opened,
                 8.0,
             )
-            opened = open_gate([x1], [], [5], [4], [(over_x, 4), (over_y, 3)])
+            opened = open_gate([x1], [], [5], [3, 4], [(over_x, 4)])
             x2, entry2, cq, ckv, mixed2, lse2, branch2 = run(
                 partial(cross_kernel, words=words),
                 "cross",

time: 486 us -> 484 us (level)
  waiting for transfers between devices: 97.4 us -> 87.4 us
  local copies, waits for them, and re-layouts: 10.9 us -> 18.7 us
    unnamed x37 -> x67, local copies, waits for them, and re-layouts: 5.96 us -> 14.5 us
    ppermute x45, waiting for transfers between devices: 39.2 us -> 32.8 us  [tensor_hop(): return lax.ppermute(values, 'tensor', [(i, i ^ step) for i in range(4)])]
  transfers between devices with their start and end apart: 69 -> 69, of which waited for: 29 -> 27; matrix products, arithmetic and copies ran while one was open for 2% -> 1% of each run, Pallas kernels for 56% -> 55%
where the time goes in v2:
time: 484 us; the launch traced here: 478 us
  Pallas kernels  322 us (67%)
  waiting for transfers between devices  87.4 us (18%)
  starting transfers between devices  46.9 us (10%)
  local copies, waits for them, and re-layouts  18.7 us (4%)
    pallas_call x19, Pallas kernels, run(): pl.pallas_call(kernel, out_shape=[outs[n] for n in out_names] + [small_ou...  256 us
    ppermute x24, waiting for transfers between devices, dp_hop(): return lax.ppermute(values, 'dp', [(i, i ^ step) for i in range(size)])  54.5 us
    pallas_call x8, Pallas kernels, advance(): pl.pallas_call(partial(merge_kernel, spots=spots, after=len(after)), grid...  34.4 us
    ppermute x45, waiting for transfers between devices, tensor_hop(): return lax.ppermute(values, 'tensor', [(i, i ^ step) for i in range(4)])  32.8 us
    ppermute x24, starting transfers between devices, dp_hop(): return lax.ppermute(values, 'dp', [(i, i ^ step) for i in range(size)])  26.9 us
    pallas_call x8, Pallas kernels, plain(): pl.pallas_call(lambda *refs: body(*refs[:first], *refs[first + len(after)...  22.4 us
    ppermute x45, starting transfers between devices, tensor_hop(): return lax.ppermute(values, 'tensor', [(i, i ^ step) for i in range(4)])  20 us
    unnamed x67, local copies, waits for them, and re-layouts  14.5 us
  transfers between devices with their start and end apart: 69, of which 27 were waited for; matrix products, arithmetic and copies ran while one was open for 1% of the time, Pallas kernels for 55%

profile of v2, /device:TPU:0, one launch (start us, length us, event | category | flops | bytes accessed | tf_op | source)
XLA Modules:
  0.0 477.9 jit_solution(15011113174959835601)
XLA Ops:
  16.9 5.7 %pack_weights.2 = (bf16[768,768]{1,0:T(8,128)(2,1)}, bf16[768,768]{1,0:T(8,128)(2,1)}, bf16[768,768]{1,0:T(8,128)(2,1)}, bf16[384,768]{1,0:T(8,128)(2,1)}, bf16[...) custom-call(s32[9]{0:T(128)} %concatenate.6.info.refs_0_, ...), custom_call_target="tpu_custom_call" | custom-call | flops 400000000 | bytes 1000 | tf_op jit(solution)/shard_map/pack_weights/pallas_call | solution.py:1309
  29.3 9.7 %collective-permute-done.6.refs_0_ = bf16[384,768]{1,0:T(8,128)(2,1)S(1)} collective-permute-done((bf16[384,768]{1,0:T(8,128)(2,1)}, bf16[384,768]{1,0:T(8,128)(2,1)S(1)}, u32[]{:S(2)}, u32[]{:S(2)}) %collective-permute-start.6) | collective-permute-done | bytes 589856 | tf_op jit(solution)/shard_map/ppermute | solution.py:1246
  48.3 6.6 %self_kv.1 = (bf16[512,768]{1,0:T(8,128)(2,1)}, bf16[2,512,768]{2,1,0:T(8,128)(2,1)}, f32[512,768]{1,0:T(8,128)}) custom-call(s32[9]{0:T(128)} %concatenate.6.info.refs_0_, f32[2,4,6912]{2,1,0:T(4,128)} %get-tuple-element.182.refs_1_.refs_6_.refs_2_.refs_4_.refs_5_.refs_3_.refs_10_.refs_9_.refs_7_.refs_13_, ...), custom_call_target="tpu_custom_call" | custom-call | flops 1200000000 | bytes 1000 | tf_op jit(solution)/shard_map/self_kv/pallas_call | solution.py:162
  56.8 14.2 %collective-permute-done.13.refs_19_.refs_18_ = bf16[384,768]{1,0:T(8,128)(2,1)} collective-permute-done((bf16[384,768]{1,0:T(8,128)(2,1)}, bf16[384,768]{1,0:T(8,128)(2,1)}, u32[]{:S(2)}, u32[]{:S(2)}) %collective-permute-start.13) | collective-permute-done | bytes 589856 | tf_op jit(solution)/shard_map/ppermute | solution.py:1246
  82.8 26.9 %self_cross.1 = (f32[512,768]{1,0:T(8,128)}, bf16[512,768]{1,0:T(8,128)(2,1)}, bf16[512,768]{1,0:T(8,128)(2,1)}, f32[16,512]{1,0:T(8,128)}, bf16[512,768]{1,0:T(...) custom-call(s32[9]{0:T(128)} %concatenate.6.info.refs_0_, ...), custom_call_target="tpu_custom_call" | custom-call | flops 5600000000 | bytes 1000 | tf_op jit(solution)/shard_map/self_cross/pallas_call | solution.py:162
  112.4 9.8 %ff_part.1 = (bf16[512,768]{1,0:T(8,128)(2,1)}, bf16[512,768]{1,0:T(8,128)(2,1)}, bf16[512,1536]{1,0:T(8,128)(2,1)}, bf16[512,1536]{1,0:T(8,128)(2,1)}) custom-call(s32[9]{0:T(128)} %concatenate.6.info.refs_0_, f32[512,768]{1,0:T(8,128)} %get-tuple-element.195.refs_2_.refs_1_.refs_3_.refs_12_, ...), custom_call_target="tpu_custom_call" | custom-call | flops 2000000000 | bytes 1000 | tf_op jit(solution)/shard_map/ff_part/pallas_call | solution.py:162
  127.9 14.3 %collective-permute-done.18.refs_2_ = bf16[512,768]{1,0:T(8,128)(2,1)S(1)} collective-permute-done((bf16[512,768]{1,0:T(8,128)(2,1)}, bf16[512,768]{1,0:T(8,128)(2,1)S(1)}, u32[]{:S(2)}, u32[]{:S(2)}) %collective-permute-start.18) | collective-permute-done | bytes 786464 | tf_op jit(solution)/shard_map/ppermute | solution.py:1241
  143.9 7.8 %residual_kv.1 = (bf16[512,768]{1,0:T(8,128)(2,1)}, bf16[2,512,768]{2,1,0:T(8,128)(2,1)}, f32[512,768]{1,0:T(8,128)}, bf16[512,768]{1,0:T(8,128)(2,1)}) custom-call(s32[9]{0:T(128)} %concatenate.6.info.refs_0_, bf16[512,768]{1,0:T(8,128)(2,1)} %get-tuple-element.199.refs_4_.refs_1_, bf16[512,768]{1,0:T(8,128)(2,1)} %copy-done.20, ...), custom_call_target="tpu_custom_call" | custom-call | flops 1200000000 | bytes 1000 | tf_op jit(solution)/shard_map/residual_kv/pallas_call | solution.py:162
  163.3 17.1 %self.1 = (f32[512,768]{1,0:T(8,128)}, bf16[512,768]{1,0:T(8,128)(2,1)}, bf16[512,768]{1,0:T(8,128)(2,1)}, f32[16,512]{1,0:T(8,128)}, bf16[512,768]{1,0:T(8,128)(2,1)}) custom-call(s32[9]{0:T(128)} %concatenate.6.info.refs_0_, bf16[512,768]{1,0:T(8,128)(2,1)} %query.3.refs_1_.refs_5_, bf16[2,512,768]{2,1,0:T(8,128)(2,1)} %get-tuple-element.206.refs_2_.refs_6_, ...), custom_call_target="tpu_custom_call" | custom-call | flops 3200000000 | bytes 1000 | tf_op jit(solution)/shard_map/self/pallas_call | solution.py:162
  183.5 14.2 %cross.1 = (f32[512,768]{1,0:T(8,128)}, bf16[512,768]{1,0:T(8,128)(2,1)}, bf16[512,768]{1,0:T(8,128)(2,1)}, bf16[2,512,768]{2,1,0:T(8,128)(2,1)}, bf16[512,768]{...) custom-call(s32[9]{0:T(128)} %concatenate.6.info.refs_0_, ...), custom_call_target="tpu_custom_call" | custom-call | flops 2400000000 | bytes 1000 | tf_op jit(solution)/shard_map/cross/pallas_call | solution.py:162
  201.6 37.4 %ff_cross_back.1 = (bf16[768,1536]{1,0:T(8,128)(2,1)}, bf16[768,1536]{1,0:T(8,128)(2,1)}, bf16[512,768]{1,0:T(8,128)(2,1)}, bf16[768,768]{1,0:T(8,128)(2,1)}, bf...) custom-call(s32[9]{0:T(128)} %concatenate.6.info.refs_0_, ...), custom_call_target="tpu_custom_call" | custom-call | flops 4000000000 | bytes 1000 | tf_op jit(solution)/shard_map/ff_cross_back/pallas_call | solution.py:162
  239.7 26.1 %self_back.2 = (bf16[512,768]{1,0:T(8,128)(2,1)}, bf16[512,768]{1,0:T(8,128)(2,1)}, bf16[2,512,768]{2,1,0:T(8,128)(2,1)}, bf16[2,512,768]{2,1,0:T(8,128)(2,1)}, f32[72,768]{1,0:T(8,128)}) custom-call(s32[9]{0:T(128)} %concatenate.6.info.refs_0_, f32[512,768]{1,0:T(8,128)} %get-tuple-element.229.refs_1_.refs_6_, bf16[512,768]{1,0:T(8,128)(2,1)} %get-tuple-element.230.refs_2_, ...), custom_call_target="tpu_custom_call" | custom-call | flops 5200000000 | bytes 1000 | tf_op jit(solution)/shard_map/self_back/pallas_call | solution.py:162
  271.5 5.0 %qo_grads.2 = (bf16[768,384]{1,0:T(8,128)(2,1)}, bf16[768,384]{1,0:T(8,128)(2,1)}) custom-call(s32[9]{0:T(128)} %concatenate.6.info.refs_0_, bf16[512,768]{1,0:T(8,128)(2,1)} %get-tuple-element.205.refs_1_.refs_3_, bf16[512,768]{1,0:T(8,128)(2,1)} %get-tuple-element.243.refs_2_, bf16[512,768]{1,0:T(8,128)(2,1)} %get-tuple-element.239.refs_4_.refs_3_, ...), custom_call_target="tpu_custom_call" | custom-call | flops 24000000000 | bytes 1000 | tf_op jit(solution)/shard_map/qo_grads/pallas_call | solution.py:162
  276.4 12.4 %qkv_back.2 = (bf16[768,384]{1,0:T(8,128)(2,1)}, bf16[768,384]{1,0:T(8,128)(2,1)}, f32[512,768]{1,0:T(8,128)}, f32[72,768]{1,0:T(8,128)}) custom-call(s32[9]{0:T(128)} %concatenate.6.info.refs_0_, bf16[2,512,768]{2,1,0:T(8,128)(2,1)} %get-tuple-element.237.refs_1_, bf16[2,512,768]{2,1,0:T(8,128)(2,1)} %collective-permute-done.37.refs_2_, ...), custom_call_target="tpu_custom_call" | custom-call | flops 2400000000 | bytes 1000 | tf_op jit(solution)/shard_map/qkv_back/pallas_call | solution.py:162
  292.1 7.3 %collective-permute-done.39 = bf16[4,96,1536]{2,1,0:T(8,128)(2,1)} collective-permute-done((bf16[4,96,1536]{2,1,0:T(8,128)(2,1)}, bf16[4,96,1536]{2,1,0:T(8,128)(2,1)}, u32[]{:S(2)}, u32[]{:S(2)}) %collective-permute-start.39) | collective-permute-done | bytes 1179680 | tf_op jit(solution)/shard_map/ppermute | solution.py:1246
  299.3 5.8 %merge_grads.9 = (bf16[2,96,1536]{2,1,0:T(8,128)(2,1)}, bf16[2,96,1536]{2,1,0:T(8,128)(2,1)}, bf16[4,96,1536]{2,1,0:T(8,128)(2,1)}, bf16[4,96,1536]{2,1,0:T(8,128)(2,1)}) custom-call(s32[9]{0:T(128)} %concatenate.6.info.refs_0_, bf16[2,2,96,1536]{3,2,1,0:T(8,128)(2,1)} %bitcast.21.refs_0_.refs_2_, bf16[2,2,96,1536]{3,2,1,0:T(8,128)(2,1)} %bitcast.83, ...), custom_call_target="tpu_custom_call" | custom-call | flops 600000000 | bytes 1000 | tf_op jit(solution)/shard_map/merge_grads/pallas_call | solution.py:1682
  305.7 10.8 %ff_back.1 = (bf16[512,768]{1,0:T(8,128)(2,1)}, bf16[512,768]{1,0:T(8,128)(2,1)}, bf16[512,1536]{1,0:T(8,128)(2,1)}, f32[72,768]{1,0:T(8,128)}) custom-call(s32[9]{0:T(128)} %concatenate.6.info.refs_0_, f32[512,768]{1,0:T(8,128)} %get-tuple-element.245.refs_16_.refs_1_, bf16[512,768]{1,0:T(8,128)(2,1)} %get-tuple-element.246.refs_2_, ...), custom_call_target="tpu_custom_call" | custom-call | flops 2000000000 | bytes 1000 | tf_op jit(solution)/shard_map/ff_back/pallas_call | solution.py:162
  320.5 7.4 %ff_grads.1 = (bf16[768,1536]{1,0:T(8,128)(2,1)}, bf16[768,1536]{1,0:T(8,128)(2,1)}) custom-call(s32[9]{0:T(128)} %concatenate.6.info.refs_0_, bf16[512,768]{1,0:T(8,128)(2,1)} %get-tuple-element.265.refs_1_, bf16[512,1536]{1,0:T(8,128)(2,1)} %get-tuple-element.266.refs_2_, bf16[512,768]{1,0:T(8,128)(2,1)} %get-tuple-element.255.refs_3_.refs_5_, ...), custom_call_target="tpu_custom_call" | custom-call | flops 400000000 | bytes 1000 | tf_op jit(solution)/shard_map/ff_grads/pallas_call | solution.py:162
  343.5 19.3 %cross_back.1 = (bf16[768,768]{1,0:T(8,128)(2,1)}, bf16[768,768]{1,0:T(8,128)(2,1)}, f32[512,768]{1,0:T(8,128)}, f32[72,768]{1,0:T(8,128)}) custom-call(s32[9]{0:T(128)} %concatenate.6.info.refs_0_, f32[512,768]{1,0:T(8,128)} %get-tuple-element.245.refs_16_.refs_1_, bf16[512,768]{1,0:T(8,128)(2,1)} %get-tuple-element.256.refs_2_, ...), custom_call_target="tpu_custom_call" | custom-call | flops 24000000000 | bytes 1000 | tf_op jit(solution)/shard_map/cross_back/pallas_call | solution.py:162
  363.8 5.2 %merge_grads.11 = (bf16[4,96,1536]{2,1,0:T(8,128)(2,1)}, bf16[4,96,1536]{2,1,0:T(8,128)(2,1)}, bf16[1,96,1536]{2,1,0:T(8,128)(2,1)}, bf16[1,96,1536]{2,1,0:T(8,128)(2,1)}) custom-call(s32[9]{0:T(128)} %concatenate.6.info.refs_0_, bf16[4,2,96,1536]{3,2,1,0:T(8,128)(2,1)} %bitcast.34.refs_0_.refs_2_, bf16[4,2,96,1536]{3,2,1,0:T(8,128)(2,1)} %bitcast.74, ...), custom_call_target="tpu_custom_call" | custom-call | flops 600000000 | bytes 1000 | tf_op jit(solution)/shard_map/merge_grads/pallas_call | solution.py:1682
  369.8 26.2 %self_back.3 = (bf16[512,768]{1,0:T(8,128)(2,1)}, bf16[512,768]{1,0:T(8,128)(2,1)}, bf16[2,512,768]{2,1,0:T(8,128)(2,1)}, bf16[2,512,768]{2,1,0:T(8,128)(2,1)}, f32[72,768]{1,0:T(8,128)}) custom-call(s32[9]{0:T(128)} %concatenate.6.info.refs_0_, f32[512,768]{1,0:T(8,128)} %get-tuple-element.273.refs_8_.refs_1_.refs_4_, ...), custom_call_target="tpu_custom_call" | custom-call | flops 5200000000 | bytes 1000 | tf_op jit(solution)/shard_map/self_back/pallas_call | solution.py:162
  404.4 4.9 %qo_grads.3 = (bf16[768,384]{1,0:T(8,128)(2,1)}, bf16[768,384]{1,0:T(8,128)(2,1)}) custom-call(s32[9]{0:T(128)} %concatenate.6.info.refs_0_, bf16[512,768]{1,0:T(8,128)(2,1)} %get-tuple-element.186.refs_1_.refs_3_, bf16[512,768]{1,0:T(8,128)(2,1)} %get-tuple-element.287.refs_2_, bf16[512,768]{1,0:T(8,128)(2,1)} %get-tuple-element.288.refs_8_.refs_3_.refs_2_, ...), custom_call_target="tpu_custom_call" | custom-call | flops 24000000000 | bytes 1000 | tf_op jit(solution)/shard_map/qo_grads/pallas_call | solution.py:162
  409.4 5.8 %kv_grads.1 = (bf16[768,384]{1,0:T(8,128)(2,1)}, bf16[768,384]{1,0:T(8,128)(2,1)}, bf16[2,512,768]{2,1,0:T(8,128)(2,1)}) custom-call(s32[9]{0:T(128)} %concatenate.6.info.refs_0_, bf16[2,512,768]{2,1,0:T(8,128)(2,1)} %get-tuple-element.285.refs_1_, bf16[2,512,768]{2,1,0:T(8,128)(2,1)} %collective-permute-done.49.refs_2_, ...), custom_call_target="tpu_custom_call" | custom-call | flops 1600000000 | bytes 1000 | tf_op jit(solution)/shard_map/kv_grads/pallas_call | solution.py:162
  427.7 9.6 %qkv_back.3 = (bf16[512,768]{1,0:T(8,128)(2,1)}, f32[512,768]{1,0:T(8,128)}, f32[72,768]{1,0:T(8,128)}) custom-call(s32[9]{0:T(128)} %concatenate.6.info.refs_0_, bf16[2,512,768]{2,1,0:T(8,128)(2,1)} %get-tuple-element.295.refs_1_, bf16[512,768]{1,0:T(8,128)(2,1)} %get-tuple-element.288.refs_8_.refs_3_.refs_2_, ...), custom_call_target="tpu_custom_call" | custom-call | flops 2400000000 | bytes 1000 | tf_op jit(solution)/shard_map/qkv_back/pallas_call | solution.py:162
  (245 shorter events, 166.9 us)
Async XLA Ops:
  8.5 39.0 %collective-permute-start.10 = (bf16[2,768,768]{2,1,0:T(8,128)(2,1)}, bf16[2,768,768]{2,1,0:T(8,128)(2,1)}, u32[]{:S(2)}, u32[]{:S(2)}) collective-permute-start(bf16[2,768,768]{2,1,0:T(8,128)(2,1)} %refs_5_.3), channel_id=1, source_target_pairs={{0,1},{1,0},{2,3},{3,2},{4,5},{5,4},{6,7},{7,6},{8,9},{9,8},{10,11... | collective-permute-start | bytes 7077896 | tf_op jit(solution)/shard_map/ppermute | solution.py:1241
  8.5 39.0 %collective-permute-start.11 = (bf16[2,768,768]{2,1,0:T(8,128)(2,1)}, bf16[2,768,768]{2,1,0:T(8,128)(2,1)}, u32[]{:S(2)}, u32[]{:S(2)}) collective-permute-start(bf16[2,768,768]{2,1,0:T(8,128)(2,1)} %refs_7_.5), channel_id=1, source_target_pairs={{0,1},{1,0},{2,3},{3,2},{4,5},{5,4},{6,7},{7,6},{8,9},{9,8},{10,11... | collective-permute-start | bytes 7077896 | tf_op jit(solution)/shard_map/ppermute | solution.py:1241
  55.0 27.8 %collective-permute-start.12 = (bf16[2,512,768]{2,1,0:T(8,128)(2,1)}, bf16[2,512,768]{2,1,0:T(8,128)(2,1)}, u32[]{:S(2)}, u32[]{:S(2)}) collective-permute-start(bf16[2,512,768]{2,1,0:T(8,128)(2,1)} %get-tuple-element.187.refs_2_.refs_6_), channel_id=1, source_target_pairs={{0,1},{1,0},{2,3},{3,2},{4,5},{5,4},{6,7},{7,6},{8,9},{9,8},{10,11... | collective-permute-start | bytes 4718600 | tf_op jit(solution)/shard_map/ppermute | solution.py:1241
  71.1 52.5 %collective-permute-start.22 = (bf16[768,768]{1,0:T(8,128)(2,1)}, bf16[768,768]{1,0:T(8,128)(2,1)}, u32[]{:S(2)}, u32[]{:S(2)}) collective-permute-start(bf16[768,768]{1,0:T(8,128)(2,1)} %get-tuple-element.200.refs_8_.refs_3_.refs_7_.refs_11_.refs_9_), channel_id=1, source_target_pairs={{0,1},{1,0},{2,3},{3,2},{4,5},{5,4},{6,7},{7,6},{8,9},{9,8},{10,11... | collective-permute-start | bytes 3538952 | tf_op jit(solution)/shard_map/ppermute | solution.py:1241
  74.9 34.8 %collective-permute-start.16 = (bf16[384,768]{1,0:T(8,128)(2,1)}, bf16[384,768]{1,0:T(8,128)(2,1)S(1)}, u32[]{:S(2)}, u32[]{:S(2)}) collective-permute-start(bf16[384,768]{1,0:T(8,128)(2,1)} %get-tuple-element.192.refs_22_), channel_id=1, source_target_pairs={{0,2},{1,3},{2,0},{3,1},{4,6},{5,7},{6,4},{7,5},{8,10},{9,11},{10,... | collective-permute-start | bytes 1769480 | tf_op jit(solution)/shard_map/ppermute | solution.py:1241
  76.3 33.4 %collective-permute-start.17 = (bf16[384,768]{1,0:T(8,128)(2,1)}, bf16[384,768]{1,0:T(8,128)(2,1)}, u32[]{:S(2)}, u32[]{:S(2)}) collective-permute-start(bf16[384,768]{1,0:T(8,128)(2,1)} %get-tuple-element.193.refs_23_), channel_id=1, source_target_pairs={{0,2},{1,3},{2,0},{3,1},{4,6},{5,7},{6,4},{7,5},{8,10},{9,11},{10,... | collective-permute-start | bytes 1769480 | tf_op jit(solution)/shard_map/ppermute | solution.py:1241
  81.2 42.4 %collective-permute-start.19 = (bf16[384,768]{1,0:T(8,128)(2,1)}, bf16[384,768]{1,0:T(8,128)(2,1)}, u32[]{:S(2)}, u32[]{:S(2)}) collective-permute-start(bf16[384,768]{1,0:T(8,128)(2,1)} %get-tuple-element.194.refs_24_), channel_id=1, source_target_pairs={{0,2},{1,3},{2,0},{3,1},{4,6},{5,7},{6,4},{7,5},{8,10},{9,11},{10,... | collective-permute-start | bytes 1769480 | tf_op jit(solution)/shard_map/ppermute | solution.py:1241
  126.7 25.9 %collective-permute-start.26 = (bf16[768,768]{1,0:T(8,128)(2,1)}, bf16[768,768]{1,0:T(8,128)(2,1)}, u32[]{:S(2)}, u32[]{:S(2)}) collective-permute-start(bf16[768,768]{1,0:T(8,128)(2,1)} %get-tuple-element.209.refs_6_.refs_26_), channel_id=1, source_target_pairs={{0,1},{1,0},{2,3},{3,2},{4,5},{5,4},{6,7},{7,6},{8,9},{9,8},{10,11... | collective-permute-start | bytes 3538952 | tf_op jit(solution)/shard_map/ppermute | solution.py:1241
  152.3 28.0 %collective-permute-start.28 = (bf16[384,768]{1,0:T(8,128)(2,1)}, bf16[384,768]{1,0:T(8,128)(2,1)S(1)}, u32[]{:S(2)}, u32[]{:S(2)}) collective-permute-start(bf16[384,768]{1,0:T(8,128)(2,1)} %get-tuple-element.198.refs_9_.refs_8_.refs_28_), channel_id=1, source_target_pairs={{0,4},{4,0},{8,12},{12,8},{16,20},{20,16},{24,28},{28,24},{1,5},{5... | collective-permute-start | bytes 1769480 | tf_op jit(solution)/shard_map/ppermute | solution.py:1246
  152.6 27.7 %collective-permute-start.30 = (bf16[384,768]{1,0:T(8,128)(2,1)}, bf16[384,768]{1,0:T(8,128)(2,1)}, u32[]{:S(2)}, u32[]{:S(2)}) collective-permute-start(bf16[384,768]{1,0:T(8,128)(2,1)} %get-tuple-element.204.refs_14_.refs_15_), channel_id=1, source_target_pairs={{0,1},{1,0},{2,3},{3,2},{4,5},{5,4},{6,7},{7,6},{8,9},{9,8},{10,11... | collective-permute-start | bytes 1769480 | tf_op jit(solution)/shard_map/ppermute | solution.py:1241
  152.6 28.0 %collective-permute-start.29 = (bf16[384,768]{1,0:T(8,128)(2,1)}, bf16[384,768]{1,0:T(8,128)(2,1)}, u32[]{:S(2)}, u32[]{:S(2)}) collective-permute-start(bf16[384,768]{1,0:T(8,128)(2,1)} %get-tuple-element.204.refs_14_.refs_15_), channel_id=1, source_target_pairs={{0,4},{4,0},{8,12},{12,8},{16,20},{20,16},{24,28},{28,24},{1,5},{5... | collective-permute-start | bytes 1769480 | tf_op jit(solution)/shard_map/ppermute | solution.py:1246
  157.6 23.0 %collective-permute-start.27 = (bf16[384,768]{1,0:T(8,128)(2,1)}, bf16[384,768]{1,0:T(8,128)(2,1)}, u32[]{:S(2)}, u32[]{:S(2)}) collective-permute-start(bf16[384,768]{1,0:T(8,128)(2,1)} %get-tuple-element.210.refs_13_), channel_id=1, source_target_pairs={{0,2},{1,3},{2,0},{3,1},{4,6},{5,7},{6,4},{7,5},{8,10},{9,11},{10,... | collective-permute-start | bytes 1769480 | tf_op jit(solution)/shard_map/ppermute | solution.py:1241
  239.0 27.3 %collective-permute-start.38 = (bf16[768,1536]{1,0:T(8,128)(2,1)}, bf16[768,1536]{1,0:T(8,128)(2,1)}, u32[]{:S(2)}, u32[]{:S(2)}) collective-permute-start(bf16[768,1536]{1,0:T(8,128)(2,1)} %get-tuple-element.241), channel_id=1, source_target_pairs={{0,1},{1,0},{2,3},{3,2},{4,5},{5,4},{6,7},{7,6},{8,9},{9,8},{10,11... | collective-permute-start | bytes 7077896 | tf_op jit(solution)/shard_map/ppermute | solution.py:1241
  239.6 49.8 %collective-permute-start.40 = (bf16[768,768]{1,0:T(8,128)(2,1)}, bf16[768,768]{1,0:T(8,128)(2,1)}, u32[]{:S(2)}, u32[]{:S(2)}) collective-permute-start(bf16[768,768]{1,0:T(8,128)(2,1)} %get-tuple-element.249), channel_id=1, source_target_pairs={{0,1},{1,0},{2,3},{3,2},{4,5},{5,4},{6,7},{7,6},{8,9},{9,8},{10,11... | collective-permute-start | bytes 3538952 | tf_op jit(solution)/shard_map/ppermute | solution.py:1241
  271.1 28.3 %collective-permute-start.39 = (bf16[4,96,1536]{2,1,0:T(8,128)(2,1)}, bf16[4,96,1536]{2,1,0:T(8,128)(2,1)}, u32[]{:S(2)}, u32[]{:S(2)}) collective-permute-start(bf16[4,96,1536]{2,1,0:T(8,128)(2,1)} %get-tuple-element.248), channel_id=1, source_target_pairs={{0,4},{4,0},{8,12},{12,8},{16,20},{20,16},{24,28},{28,24},{1,5},{5... | collective-permute-start | bytes 3538952 | tf_op jit(solution)/shard_map/ppermute | solution.py:1246
  305.1 29.5 %collective-permute-start.45 = (bf16[4,96,1536]{2,1,0:T(8,128)(2,1)}, bf16[4,96,1536]{2,1,0:T(8,128)(2,1)}, u32[]{:S(2)}, u32[]{:S(2)}) collective-permute-start(bf16[4,96,1536]{2,1,0:T(8,128)(2,1)} %get-tuple-element.270), channel_id=1, source_target_pairs={{0,4},{4,0},{8,12},{12,8},{16,20},{20,16},{24,28},{28,24},{1,5},{5... | collective-permute-start | bytes 3538952 | tf_op jit(solution)/shard_map/ppermute | solution.py:1246
  305.7 22.2 %collective-permute-start.36 = (bf16[512,768]{1,0:T(8,128)(2,1)}, bf16[512,768]{1,0:T(8,128)(2,1)}, u32[]{:S(2)}, u32[]{:S(2)}) collective-permute-start(bf16[512,768]{1,0:T(8,128)(2,1)} %get-tuple-element.228.refs_1_), channel_id=1, source_target_pairs={{0,1},{1,0},{2,3},{3,2},{4,5},{5,4},{6,7},{7,6},{8,9},{9,8},{10,11... | collective-permute-start | bytes 2359304 | tf_op jit(solution)/shard_map/ppermute | solution.py:1241
  316.6 26.9 %collective-permute-start.43 = (bf16[512,768]{1,0:T(8,128)(2,1)}, bf16[512,768]{1,0:T(8,128)(2,1)}, u32[]{:S(2)}, u32[]{:S(2)}) collective-permute-start(bf16[512,768]{1,0:T(8,128)(2,1)} %get-tuple-element.263.refs_10_), channel_id=1, source_target_pairs={{0,2},{1,3},{2,0},{3,1},{4,6},{5,7},{6,4},{7,5},{8,10},{9,11},{10,... | collective-permute-start | bytes 2359304 | tf_op jit(solution)/shard_map/ppermute | solution.py:1241
  327.8 35.0 %collective-permute-start.46 = (bf16[768,1536]{1,0:T(8,128)(2,1)}, bf16[768,1536]{1,0:T(8,128)(2,1)}, u32[]{:S(2)}, u32[]{:S(2)}) collective-permute-start(bf16[768,1536]{1,0:T(8,128)(2,1)} %get-tuple-element.279), channel_id=1, source_target_pairs={{0,1},{1,0},{2,3},{3,2},{4,5},{5,4},{6,7},{7,6},{8,9},{9,8},{10,11... | collective-permute-start | bytes 7077896 | tf_op jit(solution)/shard_map/ppermute | solution.py:1241
  339.4 23.5 %collective-permute-start.48 = (bf16[1,96,1536]{2,1,0:T(8,128)(2,1)}, bf16[1,96,1536]{2,1,0:T(8,128)(2,1)S(1)}, u32[]{:S(2)}, u32[]{:S(2)}) collective-permute-start(bf16[1,96,1536]{2,1,0:T(8,128)(2,1)} %get-tuple-element.281), channel_id=1, source_target_pairs={{0,16},{4,20},{8,24},{12,28},{16,0},{20,4},{24,8},{28,12},{1,17},{... | collective-permute-start | bytes 884744 | tf_op jit(solution)/shard_map/ppermute | solution.py:1246
  341.9 21.0 %collective-permute-start.47 = (bf16[2,96,1536]{2,1,0:T(8,128)(2,1)}, bf16[2,96,1536]{2,1,0:T(8,128)(2,1)S(1)}, u32[]{:S(2)}, u32[]{:S(2)}) collective-permute-start(bf16[2,96,1536]{2,1,0:T(8,128)(2,1)} %get-tuple-element.280), channel_id=1, source_target_pairs={{0,8},{4,12},{8,0},{12,4},{16,24},{20,28},{24,16},{28,20},{1,9},{5... | collective-permute-start | bytes 1769480 | tf_op jit(solution)/shard_map/ppermute | solution.py:1246
  362.8 33.3 %collective-permute-start.51 = (bf16[768,768]{1,0:T(8,128)(2,1)}, bf16[768,768]{1,0:T(8,128)(2,1)}, u32[]{:S(2)}, u32[]{:S(2)}) collective-permute-start(bf16[768,768]{1,0:T(8,128)(2,1)} %get-tuple-element.290), channel_id=1, source_target_pairs={{0,1},{1,0},{2,3},{3,2},{4,5},{5,4},{6,7},{7,6},{8,9},{9,8},{10,11... | collective-permute-start | bytes 3538952 | tf_op jit(solution)/shard_map/ppermute | solution.py:1241
  368.9 28.7 %collective-permute-start.50 = (bf16[4,96,1536]{2,1,0:T(8,128)(2,1)}, bf16[4,96,1536]{2,1,0:T(8,128)(2,1)}, u32[]{:S(2)}, u32[]{:S(2)}) collective-permute-start(bf16[4,96,1536]{2,1,0:T(8,128)(2,1)} %get-tuple-element.289), channel_id=1, source_target_pairs={{0,4},{4,0},{8,12},{12,8},{16,20},{20,16},{24,28},{28,24},{1,5},{5... | collective-permute-start | bytes 3538952 | tf_op jit(solution)/shard_map/ppermute | solution.py:1246
  369.4 26.6 %collective-permute-start.52 = (bf16[1,96,1536]{2,1,0:T(8,128)(2,1)}, bf16[1,96,1536]{2,1,0:T(8,128)(2,1)S(1)}, u32[]{:S(2)}, u32[]{:S(2)}) collective-permute-start(bf16[1,96,1536]{2,1,0:T(8,128)(2,1)} %get-tuple-element.291), channel_id=1, source_target_pairs={{0,16},{4,20},{8,24},{12,28},{16,0},{20,4},{24,8},{28,12},{1,17},{... | collective-permute-start | bytes 884744 | tf_op jit(solution)/shard_map/ppermute | solution.py:1246
  (78 other events, 636.4 us)
